TPU v7x, 256 devices: a whole 4x4x8 slice. The times are simulated.
256 devices in a mesh: dp: 16 (over z_hi, x), seq: 16 (over y, z_lo, core).
Axes of the slice: x: 4, y: 4, z: 8 (z_hi: 4, z_lo: 2; z = z_hi * 2 + z_lo), core: 2. Of those that a mesh axis runs over, the one named last changes fastest.
Arguments:
- activations: bfloat16 [32768, 4096], P(('dp', 'seq')), may hold values from -24 to 24
- queries: bfloat16 [32768, 4096], P(('dp', 'seq')), may hold values from -130 to 130
- saved_keys: bfloat16 [32768, 256], P(('dp', 'seq')), may hold values from -6 to 6
- saved_values: bfloat16 [32768, 256], P(('dp', 'seq')), may hold values from -6 to 6
- output_gradient: bfloat16 [32768, 4096], P(('dp', 'seq')), may hold values from -6 to 6
- segments: int32 [16, 2048], P('dp'), may hold values from 0 to 5, never falling along the last dimension, each value on 1 to 1024 neighbouring positions
- weight_codes: int32 [4096, 512], P(('dp', 'seq')), may hold values from 32 to 215, as said below
- exponents: int32 [32, 4], replicated, may hold values from -8 to -6
Outputs:
- grad_q: bfloat16 [32768, 4096], P(('dp', 'seq'))
- grad_x: bfloat16 [32768, 4096], P(('dp', 'seq'))
- grad_weights: float32 [4096, 512], P(('dp', 'seq'))
Inputs may be any that keep to these rules, and one draw needn't show every extreme that they name: `segments`: document ids never fall along a sequence; a document holds at most 1024 positions. `weight_codes`: each code c holds an FP8 E4M3 number with sign s = c // 128, exponent field e = (c // 8) % 16 from 4 to 10 and mantissa m = c % 8.
All inputs are finite; a program needn't handle non-finite values.
Results may differ from a plain program's by a relative error of at most 0.013.
Values may be sent and summed in bfloat16 or wider, within the bound.
No kernel may reach another device: no remote copies, remote signals or barrier semaphores. Data moves between devices by JAX's collectives and lax.ppermute only.
A program may use at most 128 MiB of HBM per device.

v0:
```python
import math

import jax
import jax.numpy as jnp
from jax import lax
from jax.sharding import PartitionSpec as P

QUERY_HEADS = 32
KEY_VALUE_HEADS = 2
HEAD_WIDTH = 128
SCALE_BLOCK_SIDE = 128


masked_score = -1e30


def decode_rows(weight_codes, column_scale):
    sign_bit = (weight_codes // 128).astype(jnp.float32)
    exponent_field = (weight_codes // 8 % 16).astype(jnp.float32)
    mantissa = (weight_codes % 8).astype(jnp.float32)
    magnitude = jnp.exp2(exponent_field - 7.0) * (1.0 + mantissa / 8.0)
    return ((1.0 - 2.0 * sign_bit) * magnitude * column_scale).astype(jnp.bfloat16)


def attend_grads(query_heads, grad_heads, key_head, value_head, doc_ids, heads_dev):
    length_all = query_heads.shape[0]
    query_rows = query_heads.reshape(length_all, heads_dev, HEAD_WIDTH)
    grad_rows = grad_heads.reshape(length_all, heads_dev, HEAD_WIDTH)
    block_len = min(512, length_all)
    block_count = length_all // block_len
    score_scale = 1.0 / math.sqrt(HEAD_WIDTH)
    key_acc = jnp.zeros((length_all, HEAD_WIDTH), jnp.float32)
    value_acc = jnp.zeros((length_all, HEAD_WIDTH), jnp.float32)
    grad_blocks = []
    for block_idx in range(block_count):
        row_start = block_idx * block_len
        row_end = row_start + block_len
        query_part = query_rows[row_start:row_end]
        grad_part = grad_rows[row_start:row_end]
        key_part = key_head[:row_end]
        value_part = value_head[:row_end]
        scores = (
            jnp.einsum("qhd,kd->hqk", query_part, key_part, preferred_element_type=jnp.float32)
            * score_scale
        )
        rows_at = row_start + jnp.arange(block_len)
        cols_at = jnp.arange(row_end)
        allowed = (rows_at[:, None] >= cols_at[None, :]) & (
            doc_ids[row_start:row_end][:, None] == doc_ids[:row_end][None, :]
        )
        scores = jnp.where(allowed[None], scores, masked_score)
        row_max = jnp.max(scores, axis=-1, keepdims=True)
        exp_scores = jnp.exp(scores - row_max)
        soft_probs = exp_scores / jnp.sum(exp_scores, axis=-1, keepdims=True)
        probs_bf = soft_probs.astype(jnp.bfloat16)
        attended = jnp.einsum(
            "hqk,kd->hqd", probs_bf, value_part, preferred_element_type=jnp.float32
        )
        row_delta = jnp.sum(
            grad_part.astype(jnp.float32).transpose(1, 0, 2) * attended, axis=-1, keepdims=True
        )
        dprobs = jnp.einsum(
            "qhd,kd->hqk", grad_part, value_part, preferred_element_type=jnp.float32
        )
        dscores = (soft_probs * (dprobs - row_delta)).astype(jnp.bfloat16)
        grad_block = (
            score_scale
            * jnp.einsum("hqk,kd->qhd", dscores, key_part, preferred_element_type=jnp.float32)
        ).astype(jnp.bfloat16)
        grad_blocks.append(grad_block.reshape(block_len, heads_dev * HEAD_WIDTH))
        key_acc = key_acc.at[:row_end].add(
            score_scale
            * jnp.einsum("hqk,qhd->kd", dscores, query_part, preferred_element_type=jnp.float32)
        )
        value_acc = value_acc.at[:row_end].add(
            jnp.einsum("hqk,qhd->kd", probs_bf, grad_part, preferred_element_type=jnp.float32)
        )
    return (jnp.concatenate(grad_blocks, axis=0), key_acc, value_acc)


def on_device(
    activations,
    queries,
    saved_keys,
    saved_values,
    output_gradient,
    segments,
    weight_codes,
    exponents,
):
    seq_size = lax.axis_size("seq")
    seq_idx = lax.axis_index("seq")
    tokens_per_device = queries.shape[0]
    heads_dev = QUERY_HEADS // seq_size
    head_group = QUERY_HEADS // KEY_VALUE_HEADS
    query_heads, grad_heads = (
        lax.all_to_all(queries, "seq", split_axis=1, concat_axis=0, tiled=True),
        lax.all_to_all(output_gradient, "seq", split_axis=1, concat_axis=0, tiled=True),
    )
    keys_all, values_all = (
        lax.all_gather(saved_keys, "seq", axis=0, tiled=True),
        lax.all_gather(saved_values, "seq", axis=0, tiled=True),
    )
    kv_start = seq_idx * heads_dev // head_group * HEAD_WIDTH
    key_head = lax.dynamic_slice_in_dim(keys_all, kv_start, HEAD_WIDTH, 1)
    value_head = lax.dynamic_slice_in_dim(values_all, kv_start, HEAD_WIDTH, 1)
    doc_ids = segments[0]
    grad_query_heads, key_acc, value_acc = attend_grads(
        query_heads, grad_heads, key_head, value_head, doc_ids, heads_dev
    )
    grad_q = lax.all_to_all(grad_query_heads, "seq", split_axis=0, concat_axis=1, tiled=True)
    slot_number = seq_idx * heads_dev // head_group
    slot_selector_mask = (jnp.arange(KEY_VALUE_HEADS) == slot_number).astype(jnp.float32)
    key_totals, value_totals = (
        lax.psum_scatter(
            key_acc[:, None, :] * slot_selector_mask[None, :, None],
            "seq",
            scatter_dimension=0,
            tiled=True,
        ),
        lax.psum_scatter(
            value_acc[:, None, :] * slot_selector_mask[None, :, None],
            "seq",
            scatter_dimension=0,
            tiled=True,
        ),
    )
    kv_grad = jnp.concatenate(
        [
            key_totals.reshape(tokens_per_device, KEY_VALUE_HEADS * HEAD_WIDTH),
            value_totals.reshape(tokens_per_device, KEY_VALUE_HEADS * HEAD_WIDTH),
        ],
        axis=1,
    ).astype(jnp.bfloat16)
    rows_dev = weight_codes.shape[0]
    first_global = lax.axis_index(("dp", "seq")) * rows_dev
    row_block = (first_global + jnp.arange(rows_dev)) // SCALE_BLOCK_SIDE
    row_pick = (row_block[:, None] == jnp.arange(exponents.shape[0])[None, :]).astype(jnp.float32)
    row_scale = jnp.dot(
        row_pick, jnp.exp2(exponents.astype(jnp.float32)), precision=lax.Precision.HIGHEST
    )
    column_scale = jnp.repeat(row_scale, SCALE_BLOCK_SIDE, axis=1)
    weight_rows = decode_rows(weight_codes, column_scale)
    grad_x = jnp.einsum(
        "tc,rc->tr",
        kv_grad,
        lax.all_gather(weight_rows, ("dp", "seq"), axis=0, tiled=True),
        preferred_element_type=jnp.float32,
    ).astype(jnp.bfloat16)
    grad_weights = lax.psum_scatter(
        jnp.einsum("tr,tc->rc", activations, kv_grad, preferred_element_type=jnp.float32),
        ("dp", "seq"),
        scatter_dimension=0,
        tiled=True,
    )
    return (grad_q, grad_x, grad_weights)


def solution(mesh):
    return jax.shard_map(
        on_device,
        mesh=mesh,
        in_specs=(
            P(("dp", "seq"), None),
            P(("dp", "seq"), None),
            P(("dp", "seq"), None),
            P(("dp", "seq"), None),
            P(("dp", "seq"), None),
            P("dp", None),
            P(("dp", "seq"), None),
            P(),
        ),
        out_specs=(P(("dp", "seq"), None), P(("dp", "seq"), None), P(("dp", "seq"), None)),
        check_vma=False,
    )
```

profile of v0, /device:TPU:8, one launch (start us, length us, event | category | flops | bytes accessed | tf_op | source)
XLA Modules:
  0.0 1786.8 jit_solution(16515089712142715194)
XLA Ops:
  7.3 0.7 all-gather.4.cloned.1.call-update
  8.0 0.7 all-gather.6.cloned.1.call-update
  8.7 2.3 copy.244
  11.0 6.3 all-to-all-start
  17.7 0.7 fusion.114
  18.4 1.1 copy.243
  20.8 11.4 all-to-all-done
  32.2 6.5 all-to-all-start.1
  38.8 0.9 fusion.57
  39.7 1.3 fusion.35
  41.0 1.6 fusion.20
  42.6 1.8 fusion.14
  44.4 0.9 fusion.167
  45.4 1.1 slice.258
  46.5 1.7 slice.252
  48.3 1.7 slice.243
  50.0 4.4 all-to-all-done.1
  54.4 0.9 fusion.168
  55.3 1.0 slice.237
  56.5 1.0 slice.260
  57.5 0.9 copy.141
  58.5 0.9 copy.134
  59.4 0.9 copy.127
  60.3 3.3 fusion.187
  63.6 1.9 fusion.61
  65.5 1.1 convolution_bitcast_fusion.7
  66.6 26.2 %all-gather.6.cloned.1.call-done = bf16[2048,256]{1,0:T(8,128)(2,1)} async-done(((bf16[128,256]{1,0:T(8,128)(2,1)}), bf16[2048,256]{1,0:T(8,128)(2,1)}) %all-gather.6.cloned.1.call-update) | async-done | bytes 1048592 | tf_op jit(solution)/shard_map/all_gather | solution.py:102
  92.8 1.3 fusion.51
  94.1 2.1 fusion.32
  97.4 4.8 fusion.182
  102.3 2.9 fusion.38
  105.2 0.7 fusion.43
  106.4 0.9 copy-done.6
  107.4 0.7 fusion.11
  108.1 1.4 copy-done.4
  109.5 0.7 fusion.41
  110.2 6.5 fusion.179
  116.8 3.8 fusion.22
  120.6 1.2 fusion.29
  122.6 1.0 fusion.8
  123.6 1.7 copy-done.3
  125.3 1.0 fusion.27
  126.3 8.0 fusion.170
  134.3 4.7 fusion.16
  139.0 0.8 fusion.50
  139.8 1.3 fusion.30
  141.2 1.5 slice-done.1
  142.7 1.2 fusion.5
  143.9 1.2 fusion.24
  145.2 0.7 copy-done.1
  145.9 2.6 broadcast_multiply_fusion
  148.5 98.4 %all-reduce.6 = (bf16[2048,2,128]{2,1,0:T(2,128)(2,1)}, bf16[2048,2,128]{2,1,0:T(2,128)(2,1)}) all-reduce(f32[2048,2,128]{2,1,0:T(2,128)} %get-tuple-element.142, f32[2048,2,128]{2,1,0:T(2,128)S(1)} %get-tuple-element.141), channel_id=2, replica_groups=mesh['dp'=16,'seq'=16] {'seq'}, use_global_device_ids=true, to_apply=%region_12.13.clone | all-reduce | flops 1048576 | bytes 6291456
  246.8 1.0 dynamic-slice_convert_fusion
  247.8 4.5 convolution_bitcast_fusion
  252.4 9.1 copy.184
  261.5 1.8 fusion.45
  263.4 2.0 fusion.46
  265.4 2.6 fusion.44
  268.0 0.8 fusion.47
  269.5 21.9 %all_to_all.51 = bf16[16,128,256]{2,1,0:T(8,128)(2,1)S(1)} all-to-all(bf16[16,128,256]{2,1,0:T(8,128)(2,1)S(1)} %bitcast.262), channel_id=1, replica_groups=mesh['dp'=16,'seq'=16] {'seq'}, dimensions={0} | all-to-all | bytes 2097152 | tf_op jit(solution)/shard_map/all_to_all | solution.py:111
  292.0 1.3 copy.157
  293.3 212.2 %all-gather.8.cloned.1.call-done = bf16[4096,512]{1,0:T(8,128)(2,1)} async-done(((bf16[16,512]{1,0:T(8,128)(2,1)}), bf16[4096,512]{1,0:T(8,128)(2,1)}) %all-gather.8.cloned.1.call-update) | async-done | bytes 4194320 | tf_op jit(solution)/shard_map/all_gather | solution.py:147
  505.5 4.6 convolution_convert_fusion
  510.1 1270.1 %reduce-scatter.4.cloned.1.call-done = f32[16,512]{1,0:T(8,128)} async-done(((f32[4096,512]{1,0:T(8,128)}), f32[16,512]{1,0:T(8,128)}) %reduce-scatter.4.cloned.1.call-update) | async-done | bytes 32784
  (88 shorter events, 5.4 us)
Async XLA Ops:
  7.2 240.7 %copy-start = (bf16[128,4096]{1,0:T(8,128)(2,1)S(1)}, bf16[128,4096]{1,0:T(8,128)(2,1)}, u32[]{:S(2)}) copy-start(bf16[128,4096]{1,0:T(8,128)(2,1)} %param.28) | copy-start | bytes 3145732
  7.2 12.3 copy-start.24
  7.2 10.2 copy-start.23
  7.2 10.5 copy-start.19
  7.2 13.6 copy-start.18
  7.2 11.2 copy-start.12
  7.2 53.1 %all-gather.4.cloned.1.call-start = ((), (), s32[]{:S(2)}) async-start(), calls=%async_computation.4 | async-start | bytes 1114112 | tf_op jit(solution)/shard_map/all_gather | solution.py:101
  8.0 84.9 %all-gather.6.cloned.1.call-start = ((), (), s32[]{:S(2)}) async-start(), calls=%async_computation.5 | async-start | bytes 1114112 | tf_op jit(solution)/shard_map/all_gather | solution.py:102
  8.7 31.0 %slice-start.4 = ((s32[1,2048]{1,0:T(1,128)}), s32[1,1024]{1,0:T(1,128)S(1)}, s32[]{:S(2)}) async-start(s32[1,2048]{1,0:T(1,128)} %param.33), calls=%async_computation.12 | async-start | bytes 8192 | tf_op jit(solution)/shard_map/slice | solution.py:49
  11.0 21.2 %all-to-all-start = ((bf16[128,16,256]{2,0,1:T(8,128)(2,1)}), bf16[128,16,256]{2,0,1:T(8,128)(2,1)S(1)}, u32[]{:S(2)}, u32[]{:S(2)}) async-start(bf16[128,16,256]{2,0,1:T(8,128)(2,1)} %bitcast.255), calls=%async_computation | async-start | bytes 2097152 | tf_op jit(solution)/shard_map/all_to_all | solution.py:97
  17.3 488.2 %all-gather.8.cloned.1.call-start = ((), (), s32[]{:S(2)}) async-start(), calls=%async_computation.6 | async-start | bytes 4210688 | tf_op jit(solution)/shard_map/all_gather | solution.py:147
  32.2 22.2 %all-to-all-start.1 = ((bf16[128,16,256]{2,0,1:T(8,128)(2,1)}), bf16[128,16,256]{2,0,1:T(8,128)(2,1)S(1)}, u32[]{:S(2)}, u32[]{:S(2)}) async-start(bf16[128,16,256]{2,0,1:T(8,128)(2,1)} %bitcast.254), calls=%async_computation.1 | async-start | bytes 2097152 | tf_op jit(solution)/shard_map/all_to_all | solution.py:98
  38.7 1741.5 %reduce-scatter.4.cloned.1.call-start = ((), (), s32[]{:S(2)}) async-start(), calls=%async_computation.7 | async-start | bytes 8421376
  45.4 18.2 %copy-start.14 = (bf16[512,2,128]{2,1,0:T(2,128)(2,1)}, bf16[512,2,128]{2,1,0:T(2,128)(2,1)S(1)}, u32[]{:S(2)}) copy-start(bf16[512,2,128]{2,1,0:T(2,128)(2,1)S(1)} %slice.234) | copy-start | bytes 786436
  94.1 2.2 copy-start.15
  94.1 3.2 copy-start.13
  96.3 1.0 copy-start.7
  102.3 2.9 copy-start.17
  102.3 3.6 copy-start.20
  105.1 2.2 copy-start.6
  107.3 2.2 copy-start.16
  108.0 1.4 copy-start.4
  116.7 3.9 copy-start.11
  116.8 5.8 slice-start.2
  120.6 1.3 copy-start.21
  120.6 2.0 slice-start.3
  122.6 2.7 copy-start.9
  123.6 1.7 copy-start.3
  134.3 4.7 copy-start.10
  134.3 4.7 copy-start.22
  139.0 2.2 slice-start
  139.8 2.9 slice-start.1
  143.9 2.0 copy-start.1
  261.4 2.0 copy-start.5
  261.4 6.6 copy-start.2
  261.5 6.6 copy-start.8
Sparse Core Ops, SparseCore 0:
  9.9 46.2 all-gather.3
  58.0 34.7 all-gather.5
  94.7 410.7 all-gather.7
  508.4 1271.7 reduce-scatter.3
where the time goes:
time: 1800 us; the launch traced here: 1790 us
  waiting for transfers between devices  1530 us (85%)
  blocking collectives  120 us (7%)
  matrix products  55.2 us (3%)
  local copies, waits for them, and re-layouts  35.4 us (2%)
  other arithmetic  22.2 us (1%)
    unnamed x5, waiting for transfers between devices  1270 us
    all_gather x1, waiting for transfers between devices, on_device(): lax.all_gather(weight_rows, ('dp', 'seq'), axis=0, tiled=True)  212 us
    unnamed x1, blocking collectives  98.4 us
  transfers between devices with their start and end apart: 6, of which 5 were waited for; matrix products, arithmetic and copies ran while one was open for 6% of the time, Pallas kernels for 0%

commit v1 on v0

v1 whole, which is shorter than its diff:
```python
import math

import jax
import jax.numpy as jnp
from jax import lax
from jax.experimental import pallas as pl
from jax.experimental.pallas import tpu as pltpu
from jax.sharding import PartitionSpec as P

QUERY_HEADS = 32
KEY_VALUE_HEADS = 2
HEAD_WIDTH = 128
SCALE_BLOCK_SIDE = 128
GROUP_HEADS = QUERY_HEADS // KEY_VALUE_HEADS
GROUP_COLS = GROUP_HEADS * HEAD_WIDTH
DOC_LIMIT = 1024
HEADS_STEP = 4

masked_bias = -1e30
score_scale = 1.0 / math.sqrt(HEAD_WIDTH)
exp2_scale = score_scale * math.log2(math.e)

NT = (((1,), (1,)), ((), ()))
NN = (((1,), (0,)), ((), ()))


def dot(a, b, dims):
    return lax.dot_general(a, b, dims, preferred_element_type=jnp.float32)


def decode_rows(weight_codes, column_scale):
    sign_bit = (weight_codes // 128).astype(jnp.float32)
    exponent_field = (weight_codes // 8 % 16).astype(jnp.float32)
    mantissa = (weight_codes % 8).astype(jnp.float32)
    magnitude = jnp.exp2(exponent_field - 7.0) * (1.0 + mantissa / 8.0)
    return ((1.0 - 2.0 * sign_bit) * magnitude * column_scale).astype(jnp.bfloat16)


def attention_kernel(
    core_ref,
    q_own,
    g_own,
    q_other,
    g_other,
    kv_own,
    kv_halo,
    key_mark,
    query_mark,
    dq_own,
    dq_other,
    dkv_halo,
    dkv_own,
    ka,
    kt,
    va,
    qa,
    ga,
    s_scr,
    d_scr,
    p_scr,
    ds_scr,
    dk_acc,
    dv_acc,
):
    slot = pl.program_id(0)
    step = pl.program_id(1)
    steps = pl.num_programs(1)
    rows = HEADS_STEP * HEAD_WIDTH
    blocks = DOC_LIMIT // 128 + 1

    @pl.when((slot == 0) & (step == 0))
    def _():
        ka[:, 128:] = key_mark[...]
        for i in range(DOC_LIMIT // 256 + 1):
            block = kv_halo[i] if i < DOC_LIMIT // 256 else kv_own[...]
            at = slice(i * 256, (i + 1) * 256)
            ka[at, :128] = block[:, :128]
            va[at, :] = block[:, 128:]
            kt[:, at] = block[:, :128].T
        dk_acc[...] = jnp.zeros_like(dk_acc)
        dv_acc[...] = jnp.zeros_like(dv_acc)

    @pl.when(step == 0)
    def _():
        for h in range(HEADS_STEP):
            qa[h * 128 : (h + 1) * 128, 128:] = query_mark[0]

    @pl.when(slot == 0)
    def _():
        for h in range(HEADS_STEP):
            qa[h * 128 : (h + 1) * 128, :128] = q_own[:, h * 128 : (h + 1) * 128]
            ga[h * 128 : (h + 1) * 128, :] = g_own[:, h * 128 : (h + 1) * 128]

    @pl.when(slot == 1)
    def _():
        for h in range(HEADS_STEP):
            qa[h * 128 : (h + 1) * 128, :128] = q_other[:, h * 128 : (h + 1) * 128]
            ga[h * 128 : (h + 1) * 128, :] = g_other[:, h * 128 : (h + 1) * 128]

    half = (core_ref[0] + slot) % 2
    first = pl.multiple_of(half * 128, 128)
    q_all = qa[...]
    g_all = ga[...]

    best = jnp.full((8, rows), masked_bias, jnp.float32)
    for b in range(blocks):
        at = pl.ds(pl.multiple_of(first + b * 128, 128), 128)
        s = dot(ka[at, :], q_all, NT)
        if b == blocks - 1:
            key_at = lax.broadcasted_iota(jnp.int32, (128, rows), 0)
            query_at = lax.broadcasted_iota(jnp.int32, (128, rows), 1) % 128
            s = jnp.where(key_at <= query_at, s, masked_bias)
        s_scr[b * 128 : (b + 1) * 128, :] = s
        best = jnp.maximum(best, jnp.max(s.reshape(16, 8, rows), axis=0))
        d_scr[b * 128 : (b + 1) * 128, :] = dot(va[at, :], g_all, NT)
    row_max = jnp.max(best, axis=0, keepdims=True) * exp2_scale
    total = jnp.zeros((8, rows), jnp.float32)
    for b in range(blocks):
        here = slice(b * 128, (b + 1) * 128)
        e = jnp.exp2(s_scr[here, :] * exp2_scale - row_max)
        s_scr[here, :] = e
        total = total + jnp.sum(e.reshape(16, 8, rows), axis=0)
    inverse = 1.0 / jnp.sum(total, axis=0, keepdims=True)
    delta = jnp.zeros((8, rows), jnp.float32)
    for b in range(blocks):
        here = slice(b * 128, (b + 1) * 128)
        p = s_scr[here, :] * inverse
        s_scr[here, :] = p
        p_bf = p.astype(jnp.bfloat16)
        p_scr[here, :] = p_bf
        term = p_bf.astype(jnp.float32) * d_scr[here, :]
        delta = delta + jnp.sum(term.reshape(16, 8, rows), axis=0)
    row_delta = jnp.sum(delta, axis=0, keepdims=True)
    for b in range(blocks):
        here = slice(b * 128, (b + 1) * 128)
        ds_scr[here, :] = (s_scr[here, :] * (d_scr[here, :] - row_delta)).astype(jnp.bfloat16)
    window = pl.ds(first, blocks * 128)
    dv_acc[window, :] += dot(p_scr[...], g_all, NN)
    dk_acc[window, :] += dot(ds_scr[...], q_all[:, :128], NN)
    dq_t = dot(kt[:, window], ds_scr[...], NN) * score_scale

    @pl.when(slot == 0)
    def _():
        for h in range(HEADS_STEP):
            at = slice(h * 128, (h + 1) * 128)
            dq_own[:, at] = dq_t[:, at].T.astype(jnp.bfloat16)

    @pl.when(slot == 1)
    def _():
        for h in range(HEADS_STEP):
            at = slice(h * 128, (h + 1) * 128)
            dq_other[:, at] = dq_t[:, at].T.astype(jnp.bfloat16)

    @pl.when((slot == 1) & (step == steps - 1))
    def _():
        for i in range(DOC_LIMIT // 256):
            at = slice(i * 256, (i + 1) * 256)
            dkv_halo[i, :, :128] = (dk_acc[at, :] * score_scale).astype(jnp.bfloat16)
            dkv_halo[i, :, 128:] = dv_acc[at, :].astype(jnp.bfloat16)
        dkv_own[:, :128] = dk_acc[DOC_LIMIT:, :] * score_scale
        dkv_own[:, 128:] = dv_acc[DOC_LIMIT:, :]


def attend_grads(core, queries, grads, q_other, g_other, kv_own, kv_halo, key_mark, query_mark):
    steps = GROUP_HEADS // HEADS_STEP
    width = HEADS_STEP * HEAD_WIDTH
    rows = width
    window = DOC_LIMIT + 256
    keys = DOC_LIMIT + 128
    bf16, f32 = jnp.bfloat16, jnp.float32

    def own_in(s, j, c):
        return (0, c[0] * steps + jnp.where(s == 0, j, steps - 1))

    def own_out(s, j, c):
        return (0, jnp.where(s == 0, j, steps - 1))

    def other(s, j, c):
        return (0, jnp.where(s == 0, 0, j))

    def fixed(rank):
        return lambda s, j, c: (0,) * rank

    return pl.pallas_call(
        attention_kernel,
        grid_spec=pltpu.PrefetchScalarGridSpec(
            num_scalar_prefetch=1,
            grid=(2, steps),
            in_specs=[
                pl.BlockSpec((128, width), own_in),
                pl.BlockSpec((128, width), own_in),
                pl.BlockSpec((128, width), other),
                pl.BlockSpec((128, width), other),
                pl.BlockSpec((256, 256), fixed(2)),
                pl.BlockSpec((DOC_LIMIT // 256, 256, 256), fixed(3)),
                pl.BlockSpec((window, 128), fixed(2)),
                pl.BlockSpec((1, 128, 128), lambda s, j, c: (s, 0, 0)),
            ],
            out_specs=[
                pl.BlockSpec((128, width), own_out),
                pl.BlockSpec((128, width), other),
                pl.BlockSpec((DOC_LIMIT // 256, 256, 256), fixed(3)),
                pl.BlockSpec((256, 256), fixed(2)),
            ],
            scratch_shapes=[
                pltpu.VMEM((window, 256), bf16),
                pltpu.VMEM((128, window), bf16),
                pltpu.VMEM((window, 128), bf16),
                pltpu.VMEM((rows, 256), bf16),
                pltpu.VMEM((rows, 128), bf16),
                pltpu.VMEM((keys, rows), f32),
                pltpu.VMEM((keys, rows), f32),
                pltpu.VMEM((keys, rows), bf16),
                pltpu.VMEM((keys, rows), bf16),
                pltpu.VMEM((window, 128), f32),
                pltpu.VMEM((window, 128), f32),
            ],
        ),
        out_shape=[
            jax.ShapeDtypeStruct((128, GROUP_COLS), bf16),
            jax.ShapeDtypeStruct((128, GROUP_COLS), bf16),
            jax.ShapeDtypeStruct((DOC_LIMIT // 256, 256, 256), bf16),
            jax.ShapeDtypeStruct((256, 256), f32),
        ],
        compiler_params=pltpu.CompilerParams(
            dimension_semantics=("arbitrary", "arbitrary"), vmem_limit_bytes=40 * 1024 * 1024
        ),
        cost_estimate=pl.CostEstimate(
            flops=12 * 2 * 16 * 128 * keys * 128,
            bytes_accessed=5 << 20,
            transcendentals=32 * 128 * keys,
        ),
    )(core, queries, grads, q_other, g_other, kv_own, kv_halo, key_mark, query_mark)


def on_device(
    activations,
    queries,
    saved_keys,
    saved_values,
    output_gradient,
    segments,
    weight_codes,
    exponents,
):
    bf16, f32 = jnp.bfloat16, jnp.float32
    dp_size, seq_size = lax.axis_size("dp"), lax.axis_size("seq")
    dp_idx, seq_idx = lax.axis_index("dp"), lax.axis_index("seq")
    core = seq_idx % 2
    chip = seq_idx // 2
    chips = seq_size // 2
    same_core = [[2 * k + c for k in range(chips)] for c in range(2)]
    swap_cores = [(i, i ^ 1) for i in range(seq_size)]
    halo_chips = DOC_LIMIT // 256

    def head_cols(array, which, width):
        return lax.dynamic_slice_in_dim(array, which * width, width, 1)

    kv_mine = jnp.concatenate(
        [head_cols(saved_keys, core, 128), head_cols(saved_values, core, 128)], axis=1
    )
    kv_theirs = jnp.concatenate(
        [head_cols(saved_keys, 1 - core, 128), head_cols(saved_values, 1 - core, 128)], axis=1
    )
    kv_got = lax.ppermute(kv_theirs, "seq", swap_cores)
    kv_own = jnp.where(
        core == 0,
        jnp.concatenate([kv_mine, kv_got], axis=0),
        jnp.concatenate([kv_got, kv_mine], axis=0),
    )
    kv_halo = jnp.stack(
        [
            lax.ppermute(kv_own, "seq", [(i, i + 2 * d) for i in range(seq_size - 2 * d)])
            for d in range(halo_chips, 0, -1)
        ]
    )
    q_other = lax.ppermute(head_cols(queries, 1 - core, GROUP_COLS), "seq", swap_cores)
    g_other = lax.ppermute(head_cols(output_gradient, 1 - core, GROUP_COLS), "seq", swap_cores)

    docs = segments[0]
    padded = jnp.concatenate([jnp.full((DOC_LIMIT,), 127, jnp.int32), docs])
    key_docs = lax.dynamic_slice_in_dim(padded, chip * 256, DOC_LIMIT + 256, 0)
    own_docs = lax.dynamic_slice_in_dim(docs, seq_idx * 128, 128, 0)
    other_docs = lax.dynamic_slice_in_dim(docs, (seq_idx + 1 - 2 * core) * 128, 128, 0)
    lanes = jnp.arange(128, dtype=jnp.int32)
    key_mark = (key_docs[:, None] == lanes[None, :]).astype(bf16)
    query_mark = jnp.where(
        jnp.stack([own_docs, other_docs])[:, :, None] == lanes[None, None, :], 0.0, masked_bias
    ).astype(bf16)

    rows_dev = weight_codes.shape[0]
    first_global = (dp_idx * seq_size + seq_idx) * rows_dev
    row_block = (first_global + jnp.arange(rows_dev)) // SCALE_BLOCK_SIDE
    row_pick = (row_block[:, None] == jnp.arange(exponents.shape[0])[None, :]).astype(f32)
    row_scale = jnp.dot(
        row_pick, jnp.exp2(exponents.astype(f32)), precision=lax.Precision.HIGHEST
    )
    column_scale = jnp.repeat(row_scale, SCALE_BLOCK_SIDE, axis=1)
    weight_rows = decode_rows(weight_codes, column_scale)
    crossed = lax.ppermute(
        weight_rows,
        ("dp", "seq"),
        [
            (a * seq_size + b, b * seq_size + a)
            for a in range(dp_size)
            for b in range(seq_size)
        ],
    )
    weight_block = lax.all_gather(crossed, "dp", axis=0, tiled=True)

    tokens = activations.shape[0]
    piece = activations.shape[1] // (dp_size * seq_size)
    act_rows = (
        activations.T.reshape(dp_size, seq_size, piece, tokens)
        .transpose(1, 0, 2, 3)
        .reshape(seq_size, dp_size * piece, tokens)
    )
    act_rows, _ = lax.optimization_barrier((act_rows, kv_halo))
    act_all = lax.all_to_all(act_rows, "seq", split_axis=0, concat_axis=0)
    act_all = act_all.transpose(1, 0, 2).reshape(dp_size * piece, seq_size * tokens)

    dq_own, dq_other, dkv_halo, dkv_own = attend_grads(
        core.reshape(1), queries, output_gradient, q_other, g_other, kv_own, kv_halo,
        key_mark, query_mark,
    )
    dq_back = lax.ppermute(dq_other, "seq", swap_cores)
    grad_q = jnp.where(
        core == 0,
        jnp.concatenate([dq_own, dq_back], axis=1),
        jnp.concatenate([dq_back, dq_own], axis=1),
    )

    kv_sum = dkv_own
    for d in range(1, halo_chips + 1):
        part = lax.ppermute(
            dkv_halo[halo_chips - d], "seq", [(i, i - 2 * d) for i in range(2 * d, seq_size)]
        )
        kv_sum = kv_sum + part.astype(f32)
    kv_chip = kv_sum.astype(bf16)
    kv_group = lax.all_to_all(
        jnp.broadcast_to(kv_chip[None], (chips,) + kv_chip.shape),
        "seq",
        split_axis=0,
        concat_axis=0,
        axis_index_groups=same_core,
    ).reshape(chips * 256, 256)
    kv_swap = lax.ppermute(kv_group, "seq", swap_cores)
    low = jnp.where(core == 0, kv_group, kv_swap)
    high = jnp.where(core == 0, kv_swap, kv_group)
    kv_grad = jnp.concatenate(
        [low[:, :128], high[:, :128], low[:, 128:], high[:, 128:]], axis=1
    )

    weight_part = dot(act_all, kv_grad, NN).astype(bf16)
    got = lax.all_to_all(
        weight_part.reshape(dp_size, piece, weight_part.shape[1]),
        "dp",
        split_axis=0,
        concat_axis=0,
    )
    grad_weights = jnp.sum(got.astype(f32), axis=0)
    grad_x_cols = dot(kv_grad, weight_block, NT).astype(bf16)
    grad_x = lax.all_to_all(grad_x_cols, "seq", split_axis=0, concat_axis=1, tiled=True)
    return (grad_q, grad_x, grad_weights)


def solution(mesh):
    return jax.shard_map(
        on_device,
        mesh=mesh,
        in_specs=(
            P(("dp", "seq"), None),
            P(("dp", "seq"), None),
            P(("dp", "seq"), None),
            P(("dp", "seq"), None),
            P(("dp", "seq"), None),
            P("dp", None),
            P(("dp", "seq"), None),
            P(),
        ),
        out_specs=(P(("dp", "seq"), None), P(("dp", "seq"), None), P(("dp", "seq"), None)),
        check_vma=False,
    )
```

time: 1800 us -> 204 us (0.11)
  waiting for transfers between devices: 1530 us -> 42.5 us
  blocking collectives: 120 us -> 45.6 us
  matrix products: 55.2 us -> 3.33 us
  starting transfers between devices: 13 us -> 56.5 us
  Pallas kernels: 0 us -> 31.1 us
  local copies, waits for them, and re-layouts: 35.4 us -> 15.1 us
    unnamed x5 -> x0, waiting for transfers between devices: 1270 us -> none
    all_gather x3 -> x0, waiting for transfers between devices: 238 us -> none  [the longest x1 212 us: on_device(): lax.all_gather(weight_rows, ('dp', 'seq'), axis=0, tiled=True)]
    unnamed x1 -> x0, blocking collectives: 98.4 us -> none
    all_gather x0 -> x1, blocking collectives: none -> 45.6 us  [on_device(): weight_block = lax.all_gather(crossed, 'dp', axis=0, tiled=True)]
    pallas_call x0 -> x1, Pallas kernels: none -> 31.1 us  [attend_grads(): pl.pallas_call(attention_kernel, grid_spec=pltpu.PrefetchScalarGridSpec(n...]
    dot_general x23 -> x3, matrix products: 32.6 us -> 3.33 us  [the longest x2 3.15 us: dot(): return lax.dot_general(a, b, dims, preferred_element_type=jnp.float32)]
    ppermute x0 -> x14, starting transfers between devices: none -> 26.1 us  [the longest x4 11.9 us: on_device(): lax.ppermute(kv_own, 'seq', [(i, i + 2 * d) for i in range(seq_size - 2 *...]
    sub x4 -> x0, matrix products: 22.6 us -> none  [attend_grads(): exp_scores = jnp.exp(scores - row_max)]
  transfers between devices with their start and end apart: 6 -> 18, of which waited for: 5 -> 9; matrix products, arithmetic and copies ran while one was open for 6% -> 8% of each run, Pallas kernels for 0% -> 0%
where the time goes in v1:
time: 204 us; the launch traced here: 200 us
  starting transfers between devices  56.5 us (28%)
  blocking collectives  45.6 us (22%)
  waiting for transfers between devices  42.5 us (21%)
  Pallas kernels  31.1 us (15%)
  local copies, waits for them, and re-layouts  15.1 us (7%)
  other arithmetic  5.4 us (3%)
  matrix products  3.33 us (2%)
    all_gather x1, blocking collectives, on_device(): weight_block = lax.all_gather(crossed, 'dp', axis=0, tiled=True)  45.6 us
    pallas_call x1, Pallas kernels, attend_grads(): pl.pallas_call(attention_kernel, grid_spec=pltpu.PrefetchScalarGridSpec(n...  31.1 us
    ppermute x4, starting transfers between devices, on_device(): lax.ppermute(kv_own, 'seq', [(i, i + 2 * d) for i in range(seq_size - 2 *...  11.9 us
    all_to_all x1, starting transfers between devices, on_device(): lax.all_to_all(weight_part.reshape(dp_size, piece, weight_part.shape[1]),...  11.8 us
    all_to_all x1, waiting for transfers between devices, on_device(): lax.all_to_all(grad_x_cols, 'seq', split_axis=0, concat_axis=1, tiled=True)  10.2 us
    all_to_all x1, waiting for transfers between devices, on_device(): lax.all_to_all(jnp.broadcast_to(kv_chip[None], (chips,) + kv_chip.shape),...  9.69 us
    all_to_all x1, waiting for transfers between devices, on_device(): act_all = lax.all_to_all(act_rows, 'seq', split_axis=0, concat_axis=0)  8.89 us
    ppermute x4, starting transfers between devices, on_device(): lax.ppermute(dkv_halo[halo_chips - d], 'seq', [(i, i - 2 * d) for i in ra...  8.43 us
  transfers between devices with their start and end apart: 18, of which 9 were waited for; matrix products, arithmetic and copies ran while one was open for 8% of the time, Pallas kernels for 0%

profile of v1, /device:TPU:8, one launch (start us, length us, event | category | flops | bytes accessed | tf_op | source)
XLA Modules:
  0.0 200.4 jit_solution(6472619444132766757)
XLA Ops:
  0.7 0.9 constant_dynamic-slice_fusion.4
  1.6 0.6 pad_maximum_fusion.4
  2.2 0.0 collective-permute-start.2
  2.2 1.9 constant_dynamic-slice_fusion.7
  4.1 0.5 collective-permute-start
  4.6 0.8 constant_dynamic-slice_fusion.6
  5.5 0.0 collective-permute-start.1
  5.5 0.1 pad_dynamic-slice_fusion
  5.5 0.2 fusion.key_mark
  5.8 1.0 maximum_select_fusion.1.kv_own
  6.8 4.2 %collective-permute-start.3 = (bf16[256,256]{1,0:T(8,128)(2,1)S(1)}, bf16[256,256]{1,0:T(8,128)(2,1)S(1)}, u32[]{:S(2)}, u32[]{:S(2)}) collective-permute-start(bf16[256,256]{1,0:T(8,128)(2,1)S(1)} %maximum_select_fusion.1.kv_own), channel_id=1, source_target_pairs={{0,8},{1,9},{2,10},{3,11},{4,12},{5,13},{6,14},{7,15},{16,24},{17,... | collective-permute-start | bytes 393224 | tf_op jit(solution)/shard_map/ppermute | solution.py:273
  11.0 1.9 collective-permute-start.4
  12.9 3.2 %collective-permute-start.5 = (bf16[256,256]{1,0:T(8,128)(2,1)S(1)}, bf16[256,256]{1,0:T(8,128)(2,1)S(1)}, u32[]{:S(2)}, u32[]{:S(2)}) collective-permute-start(bf16[256,256]{1,0:T(8,128)(2,1)S(1)} %maximum_select_fusion.1.kv_own), channel_id=1, source_target_pairs={{0,4},{1,5},{2,6},{3,7},{4,8},{5,9},{6,10},{7,11},{8,12},{9,13},{1... | collective-permute-start | bytes 393224 | tf_op jit(solution)/shard_map/ppermute | solution.py:273
  16.1 0.0 collective-permute-done.3
  16.2 2.6 %collective-permute-start.6 = (bf16[256,256]{1,0:T(8,128)(2,1)S(1)}, bf16[256,256]{1,0:T(8,128)(2,1)S(1)}, u32[]{:S(2)}, u32[]{:S(2)}) collective-permute-start(bf16[256,256]{1,0:T(8,128)(2,1)S(1)} %maximum_select_fusion.1.kv_own), channel_id=1, source_target_pairs={{0,2},{1,3},{2,4},{3,5},{4,6},{5,7},{6,8},{7,9},{8,10},{9,11},{10,... | collective-permute-start | bytes 393224 | tf_op jit(solution)/shard_map/ppermute | solution.py:273
  18.7 0.1 select_convert_fusion.query_mark
  18.8 4.4 %collective-permute-done.5 = bf16[256,256]{1,0:T(8,128)(2,1)S(1)} collective-permute-done((bf16[256,256]{1,0:T(8,128)(2,1)S(1)}, bf16[256,256]{1,0:T(8,128)(2,1)S(1)}, u32[]{:S(2)}, u32[]{:S(2)}) %collective-permute-start.5) | collective-permute-done | bytes 131104 | tf_op jit(solution)/shard_map/ppermute | solution.py:273
  23.2 2.3 %collective-permute-done.6 = bf16[256,256]{1,0:T(8,128)(2,1)S(1)} collective-permute-done((bf16[256,256]{1,0:T(8,128)(2,1)S(1)}, bf16[256,256]{1,0:T(8,128)(2,1)S(1)}, u32[]{:S(2)}, u32[]{:S(2)}) %collective-permute-start.6) | collective-permute-done | bytes 131104 | tf_op jit(solution)/shard_map/ppermute | solution.py:273
  25.5 0.1 pad_maximum_fusion.1.kv_halo
  25.6 0.0 copy-start.2
  25.6 0.8 copy-done.2
  26.4 0.0 collective-permute-done.1.g_other
  26.4 0.8 copy-done.4
  27.2 1.0 copy-done.3
  28.2 1.0 copy-done.5
  29.3 31.1 %shard_map.103 = (bf16[128,2048]{1,0:T(8,128)(2,1)S(1)}, bf16[128,2048]{1,0:T(8,128)(2,1)S(1)}, bf16[4,256,256]{2,1,0:T(8,128)(2,1)S(1)}, f32[256,256]{1,0:T(8,128)S(1)}) custom-call(s32[1]{0:T(128)} %bitcast.core_ref, bf16[128,4096]{1,0:T(8,128)(2,1)S(1)} %copy-done, bf16[128,4096]{1,0:T(8,128)(2,1)S(1)} %copy-done.1, bf16[128,2048]{1,0:T(8,128)(2,1)S(1)} %copy-done.3, ...), custom_call_target="tpu_custom_call" | custom-call | flops 7247757312 | bytes 5242880 | tf_op jit(solution)/shard_map/pallas_call | solution.py:184
  60.5 1.3 collective-permute-start.10
  61.8 1.3 collective-permute-start.11
  63.0 3.9 %collective-permute-start.8 = (bf16[256,256]{1,0:T(8,128)(2,1)S(1)}, bf16[256,256]{1,0:T(8,128)(2,1)S(1)}, u32[]{:S(2)}, u32[]{:S(2)}) collective-permute-start(bf16[256,256]{1,0:T(8,128)(2,1)S(1)} %get-tuple-element.19), channel_id=1, source_target_pairs={{2,0},{3,1},{4,2},{5,3},{6,4},{7,5},{8,6},{9,7},{10,8},{11,9},{12,... | collective-permute-start | bytes 393224 | tf_op jit(solution)/shard_map/ppermute | solution.py:335
  67.0 1.9 collective-permute-start.9
  68.9 1.1 collective-permute-done.10
  70.0 3.0 %collective-permute-done.11 = bf16[256,256]{1,0:T(8,128)(2,1)S(1)} collective-permute-done((bf16[256,256]{1,0:T(8,128)(2,1)S(1)}, bf16[256,256]{1,0:T(8,128)(2,1)S(1)}, u32[]{:S(2)}, u32[]{:S(2)}) %collective-permute-start.11) | collective-permute-done | bytes 131104 | tf_op jit(solution)/shard_map/ppermute | solution.py:335
  73.0 1.1 collective-permute-done.9
  74.2 0.1 add_convert_fusion
  74.3 1.0 broadcast_in_dim.14
  75.3 7.0 %all-to-all-start = ((bf16[8,256,256]{2,1,0:T(8,128)(2,1)}), bf16[8,256,256]{2,1,0:T(8,128)(2,1)S(1)}, u32[]{:S(2)}, u32[]{:S(2)}) async-start(bf16[8,256,256]{2,1,0:T(8,128)(2,1)} %broadcast_in_dim.14), calls=%async_computation | async-start | bytes 2097152 | tf_op jit(solution)/shard_map/all_to_all | solution.py:340
  82.3 1.6 copy.15
  83.9 1.2 copy.16
  85.2 9.7 %all-to-all-done = bf16[8,256,256]{2,1,0:T(8,128)(2,1)S(1)} async-done(((bf16[8,256,256]{2,1,0:T(8,128)(2,1)}), bf16[8,256,256]{2,1,0:T(8,128)(2,1)S(1)}, u32[]{:S(2)}, u32[]{:S(2)}) %all-to-all-start) | async-done | bytes 1048608 | tf_op jit(solution)/shard_map/all_to_all | solution.py:340
  94.9 5.5 %all-to-all-start.2 = ((bf16[16,256,128]{2,1,0:T(8,128)(2,1)}), bf16[16,256,128]{2,1,0:T(8,128)(2,1)S(1)}, u32[]{:S(2)}, u32[]{:S(2)}) async-start(bf16[16,256,128]{2,1,0:T(8,128)(2,1)} %bitcast.16), calls=%async_computation.2 | async-start | bytes 2097152 | tf_op jit(solution)/shard_map/all_to_all | solution.py:319
  100.4 0.1 collective-permute-start.12
  100.6 0.2 fusion.19
  100.8 0.1 broadcast_in_dim.15
  100.8 0.0 copy-done.7
  100.9 0.1 fusion.7
  100.9 5.0 %collective-permute-start.13 = (bf16[16,512]{1,0:T(8,128)(2,1)S(1)}, bf16[16,512]{1,0:T(8,128)(2,1)S(1)}, u32[]{:S(2)}, u32[]{:S(2)}) collective-permute-start(bf16[16,512]{1,0:T(8,128)(2,1)S(1)} %fusion.7), channel_id=1, source_target_pairs={{0,0},{1,16},{2,32},{3,48},{4,64},{5,80},{6,96},{7,112},{8,128},{9... | collective-permute-start | bytes 49160 | tf_op jit(solution)/shard_map/ppermute | solution.py:300
  105.9 8.9 %all-to-all-done.2 = bf16[16,256,128]{2,1,0:T(8,128)(2,1)S(1)} async-done(((bf16[16,256,128]{2,1,0:T(8,128)(2,1)}), bf16[16,256,128]{2,1,0:T(8,128)(2,1)S(1)}, u32[]{:S(2)}, u32[]{:S(2)}) %all-to-all-start.2) | async-done | bytes 1048608 | tf_op jit(solution)/shard_map/all_to_all | solution.py:319
  114.8 1.3 copy.17
  116.1 1.4 broadcast_select_fusion.1
  117.5 0.1 fusion.28
  117.6 0.0 copy-start.6
  117.6 0.1 fusion.29
  117.7 1.1 copy-done.6
  118.8 1.4 convolution_convert_fusion.1
  120.2 11.8 %all-to-all-start.3 = ((bf16[16,16,512]{2,1,0:T(8,128)(2,1)}), bf16[16,16,512]{2,1,0:T(8,128)(2,1)S(1)}, u32[]{:S(2)}, u32[]{:S(2)}) async-start(bf16[16,16,512]{2,1,0:T(8,128)(2,1)} %bitcast.41), calls=%async_computation.3 | async-start | bytes 524288 | tf_op jit(solution)/shard_map/all_to_all | solution.py:355
  132.1 45.6 %all_gather.3 = bf16[256,512]{1,0:T(8,128)(2,1)S(1)} all-gather(bf16[16,512]{1,0:T(8,128)(2,1)S(1)} %collective-permute-done.13), channel_id=1, replica_groups=mesh['dp'=16,'seq'=16] {'dp'}, dimensions={0}, use_global_device_ids=true | all-gather | bytes 278528 | tf_op jit(solution)/shard_map/all_gather | solution.py:309
  177.6 1.7 convolution_convert_fusion
  179.4 6.1 %all-to-all-start.1 = ((bf16[16,128,256]{2,1,0:T(8,128)(2,1)}), bf16[16,128,256]{2,1,0:T(8,128)(2,1)S(1)}, u32[]{:S(2)}, u32[]{:S(2)}) async-start(bf16[16,128,256]{2,1,0:T(8,128)(2,1)} %bitcast.11), calls=%async_computation.1 | async-start | bytes 2097152 | tf_op jit(solution)/shard_map/all_to_all | solution.py:363
  185.4 0.1 collective-permute-start.7
  185.6 1.8 collective-permute-done.7
  187.3 1.2 maximum_select_fusion
  188.5 0.7 convert_reduce_fusion
  189.2 10.2 %all-to-all-done.1 = bf16[16,128,256]{2,1,0:T(8,128)(2,1)S(1)} async-done(((bf16[16,128,256]{2,1,0:T(8,128)(2,1)}), bf16[16,128,256]{2,1,0:T(8,128)(2,1)S(1)}, u32[]{:S(2)}, u32[]{:S(2)}) %all-to-all-start.1) | async-done | bytes 1048608 | tf_op jit(solution)/shard_map/all_to_all | solution.py:363
  199.4 1.1 copy.19
  (23 shorter events, 0.1 us)
Async XLA Ops:
  0.6 4.0 %copy-start.1 = (bf16[128,4096]{1,0:T(8,128)(2,1)S(1)}, bf16[128,4096]{1,0:T(8,128)(2,1)}, u32[]{:S(2)}) copy-start(bf16[128,4096]{1,0:T(8,128)(2,1)} %g_own.1) | copy-start | bytes 3145732
  2.2 3.6 %collective-permute-start.2 = (bf16[128,256]{1,0:T(8,128)(2,1)}, bf16[128,256]{1,0:T(8,128)(2,1)}, u32[]{:S(2)}, u32[]{:S(2)}) collective-permute-start(bf16[128,256]{1,0:T(8,128)(2,1)} %pad_maximum_fusion.4), channel_id=1, source_target_pairs={{0,1},{1,0},{2,3},{3,2},{4,5},{5,4},{6,7},{7,6},{8,9},{9,8},{10,11... | collective-permute-start | bytes 196616 | tf_op jit(solution)/shard_map/ppermute | solution.py:265
  2.2 3.2 %copy-start.8 = (s32[1,2048]{1,0:T(1,128)S(1)}, s32[1,2048]{1,0:T(1,128)}, u32[]{:S(2)}) copy-start(s32[1,2048]{1,0:T(1,128)} %param.13) | copy-start | bytes 24580
  4.1 21.5 %collective-permute-start = (bf16[128,2048]{1,0:T(8,128)(2,1)}, bf16[128,2048]{1,0:T(8,128)(2,1)S(1)}, u32[]{:S(2)}, u32[]{:S(2)}) collective-permute-start(bf16[128,2048]{1,0:T(8,128)(2,1)} %constant_dynamic-slice_fusion.7), channel_id=1, source_target_pairs={{0,1},{1,0},{2,3},{3,2},{4,5},{5,4},{6,7},{7,6},{8,9},{9,8},{10,11... | collective-permute-start | bytes 1572872 | tf_op jit(solution)/shard_map/ppermute | solution.py:277
  5.5 21.7 %copy-start = (bf16[128,4096]{1,0:T(8,128)(2,1)S(1)}, bf16[128,4096]{1,0:T(8,128)(2,1)}, u32[]{:S(2)}) copy-start(bf16[128,4096]{1,0:T(8,128)(2,1)} %q_own.1) | copy-start | bytes 3145732
  5.5 20.9 %collective-permute-start.1 = (bf16[128,2048]{1,0:T(8,128)(2,1)}, bf16[128,2048]{1,0:T(8,128)(2,1)S(1)}, u32[]{:S(2)}, u32[]{:S(2)}) collective-permute-start(bf16[128,2048]{1,0:T(8,128)(2,1)} %constant_dynamic-slice_fusion.6), channel_id=1, source_target_pairs={{0,1},{1,0},{2,3},{3,2},{4,5},{5,4},{6,7},{7,6},{8,9},{9,8},{10,11... | collective-permute-start | bytes 1572872 | tf_op jit(solution)/shard_map/ppermute | solution.py:278
  6.8 9.4 %collective-permute-start.3 = (bf16[256,256]{1,0:T(8,128)(2,1)S(1)}, bf16[256,256]{1,0:T(8,128)(2,1)S(1)}, u32[]{:S(2)}, u32[]{:S(2)}) collective-permute-start(bf16[256,256]{1,0:T(8,128)(2,1)S(1)} %maximum_select_fusion.1.kv_own), channel_id=1, source_target_pairs={{0,8},{1,9},{2,10},{3,11},{4,12},{5,13},{6,14},{7,15},{16,24},{17,... | collective-permute-start | bytes 393224 | tf_op jit(solution)/shard_map/ppermute | solution.py:273
  11.0 7.8 %collective-permute-start.4 = (bf16[256,256]{1,0:T(8,128)(2,1)S(1)}, bf16[256,256]{1,0:T(8,128)(2,1)S(1)}, u32[]{:S(2)}, u32[]{:S(2)}) collective-permute-start(bf16[256,256]{1,0:T(8,128)(2,1)S(1)} %maximum_select_fusion.1.kv_own), channel_id=1, source_target_pairs={{0,6},{1,7},{2,8},{3,9},{4,10},{5,11},{6,12},{7,13},{8,14},{9,15},... | collective-permute-start | bytes 393224 | tf_op jit(solution)/shard_map/ppermute | solution.py:273
  12.9 10.3 %collective-permute-start.5 = (bf16[256,256]{1,0:T(8,128)(2,1)S(1)}, bf16[256,256]{1,0:T(8,128)(2,1)S(1)}, u32[]{:S(2)}, u32[]{:S(2)}) collective-permute-start(bf16[256,256]{1,0:T(8,128)(2,1)S(1)} %maximum_select_fusion.1.kv_own), channel_id=1, source_target_pairs={{0,4},{1,5},{2,6},{3,7},{4,8},{5,9},{6,10},{7,11},{8,12},{9,13},{1... | collective-permute-start | bytes 393224 | tf_op jit(solution)/shard_map/ppermute | solution.py:273
  16.2 9.4 %collective-permute-start.6 = (bf16[256,256]{1,0:T(8,128)(2,1)S(1)}, bf16[256,256]{1,0:T(8,128)(2,1)S(1)}, u32[]{:S(2)}, u32[]{:S(2)}) collective-permute-start(bf16[256,256]{1,0:T(8,128)(2,1)S(1)} %maximum_select_fusion.1.kv_own), channel_id=1, source_target_pairs={{0,2},{1,3},{2,4},{3,5},{4,6},{5,7},{6,8},{7,9},{8,10},{9,11},{10,... | collective-permute-start | bytes 393224 | tf_op jit(solution)/shard_map/ppermute | solution.py:273
  25.6 0.8 copy-start.2
  26.4 0.8 copy-start.4
  27.2 1.0 copy-start.3
  28.2 1.0 copy-start.5
  60.5 9.6 %collective-permute-start.10 = (bf16[256,256]{1,0:T(8,128)(2,1)S(1)}, bf16[256,256]{1,0:T(8,128)(2,1)S(1)}, u32[]{:S(2)}, u32[]{:S(2)}) collective-permute-start(bf16[256,256]{1,0:T(8,128)(2,1)S(1)} %get-tuple-element.21), channel_id=1, source_target_pairs={{6,0},{7,1},{8,2},{9,3},{10,4},{11,5},{12,6},{13,7},{14,8},{15,9},... | collective-permute-start | bytes 393224 | tf_op jit(solution)/shard_map/ppermute | solution.py:335
  61.8 11.3 %collective-permute-start.11 = (bf16[256,256]{1,0:T(8,128)(2,1)S(1)}, bf16[256,256]{1,0:T(8,128)(2,1)S(1)}, u32[]{:S(2)}, u32[]{:S(2)}) collective-permute-start(bf16[256,256]{1,0:T(8,128)(2,1)S(1)} %get-tuple-element.20), channel_id=1, source_target_pairs={{8,0},{9,1},{10,2},{11,3},{12,4},{13,5},{14,6},{15,7},{24,16},{25,... | collective-permute-start | bytes 393224 | tf_op jit(solution)/shard_map/ppermute | solution.py:335
  63.0 10.0 %collective-permute-start.8 = (bf16[256,256]{1,0:T(8,128)(2,1)S(1)}, bf16[256,256]{1,0:T(8,128)(2,1)S(1)}, u32[]{:S(2)}, u32[]{:S(2)}) collective-permute-start(bf16[256,256]{1,0:T(8,128)(2,1)S(1)} %get-tuple-element.19), channel_id=1, source_target_pairs={{2,0},{3,1},{4,2},{5,3},{6,4},{7,5},{8,6},{9,7},{10,8},{11,9},{12,... | collective-permute-start | bytes 393224 | tf_op jit(solution)/shard_map/ppermute | solution.py:335
  67.0 7.2 %collective-permute-start.9 = (bf16[256,256]{1,0:T(8,128)(2,1)S(1)}, bf16[256,256]{1,0:T(8,128)(2,1)S(1)}, u32[]{:S(2)}, u32[]{:S(2)}) collective-permute-start(bf16[256,256]{1,0:T(8,128)(2,1)S(1)} %get-tuple-element.22), channel_id=1, source_target_pairs={{4,0},{5,1},{6,2},{7,3},{8,4},{9,5},{10,6},{11,7},{12,8},{13,9},{1... | collective-permute-start | bytes 393224 | tf_op jit(solution)/shard_map/ppermute | solution.py:335
  75.3 19.5 %all-to-all-start = ((bf16[8,256,256]{2,1,0:T(8,128)(2,1)}), bf16[8,256,256]{2,1,0:T(8,128)(2,1)S(1)}, u32[]{:S(2)}, u32[]{:S(2)}) async-start(bf16[8,256,256]{2,1,0:T(8,128)(2,1)} %broadcast_in_dim.14), calls=%async_computation | async-start | bytes 2097152 | tf_op jit(solution)/shard_map/all_to_all | solution.py:340
  85.2 15.4 %copy-start.9 = (s32[32,4]{0,1:T(4,128)S(1)}, s32[32,4]{0,1:T(4,128)}, u32[]{:S(2)}) copy-start(s32[32,4]{0,1:T(4,128)} %param.15) | copy-start | bytes 1540
  85.2 15.7 %copy-start.7 = (s32[16,512]{1,0:T(8,128)S(1)}, s32[16,512]{1,0:T(8,128)}, u32[]{:S(2)}) copy-start(s32[16,512]{1,0:T(8,128)} %param.14) | copy-start | bytes 98308
  94.9 20.0 %all-to-all-start.2 = ((bf16[16,256,128]{2,1,0:T(8,128)(2,1)}), bf16[16,256,128]{2,1,0:T(8,128)(2,1)S(1)}, u32[]{:S(2)}, u32[]{:S(2)}) async-start(bf16[16,256,128]{2,1,0:T(8,128)(2,1)} %bitcast.16), calls=%async_computation.2 | async-start | bytes 2097152 | tf_op jit(solution)/shard_map/all_to_all | solution.py:319
  100.4 15.7 %collective-permute-start.12 = (bf16[2048,256]{1,0:T(8,128)(2,1)S(1)}, bf16[2048,256]{1,0:T(8,128)(2,1)}, u32[]{:S(2)}, u32[]{:S(2)}) collective-permute-start(bf16[2048,256]{1,0:T(8,128)(2,1)S(1)} %bitcast.35), channel_id=1, source_target_pairs={{0,1},{1,0},{2,3},{3,2},{4,5},{5,4},{6,7},{7,6},{8,9},{9,8},{10,11... | collective-permute-start | bytes 3145736 | tf_op jit(solution)/shard_map/ppermute | solution.py:347
  100.9 31.1 %collective-permute-start.13 = (bf16[16,512]{1,0:T(8,128)(2,1)S(1)}, bf16[16,512]{1,0:T(8,128)(2,1)S(1)}, u32[]{:S(2)}, u32[]{:S(2)}) collective-permute-start(bf16[16,512]{1,0:T(8,128)(2,1)S(1)} %fusion.7), channel_id=1, source_target_pairs={{0,0},{1,16},{2,32},{3,48},{4,64},{5,80},{6,96},{7,112},{8,128},{9... | collective-permute-start | bytes 49160 | tf_op jit(solution)/shard_map/ppermute | solution.py:300
  117.6 1.2 copy-start.6
  120.2 59.1 %all-to-all-start.3 = ((bf16[16,16,512]{2,1,0:T(8,128)(2,1)}), bf16[16,16,512]{2,1,0:T(8,128)(2,1)S(1)}, u32[]{:S(2)}, u32[]{:S(2)}) async-start(bf16[16,16,512]{2,1,0:T(8,128)(2,1)} %bitcast.41), calls=%async_computation.3 | async-start | bytes 524288 | tf_op jit(solution)/shard_map/all_to_all | solution.py:355
  179.4 20.0 %all-to-all-start.1 = ((bf16[16,128,256]{2,1,0:T(8,128)(2,1)}), bf16[16,128,256]{2,1,0:T(8,128)(2,1)S(1)}, u32[]{:S(2)}, u32[]{:S(2)}) async-start(bf16[16,128,256]{2,1,0:T(8,128)(2,1)} %bitcast.11), calls=%async_computation.1 | async-start | bytes 2097152 | tf_op jit(solution)/shard_map/all_to_all | solution.py:363
  185.4 1.9 collective-permute-start.7

commit v2 on v1

--- a/solution.py
+++ b/solution.py
@@ -306,7 +306,33 @@
             for b in range(seq_size)
         ],
     )
-    weight_block = lax.all_gather(crossed, "dp", axis=0, tiled=True)
+    x_size = 4
+    x_at, z_at = dp_idx % x_size, dp_idx // x_size
+    z_size = dp_size // x_size
+
+    def x_turn(d):
+        return [
+            (i, i // x_size * x_size + (i % x_size + d) % x_size) for i in range(dp_size)
+        ]
+
+    def z_turn(d):
+        return [(i, (i // x_size + d) % z_size * x_size + i % x_size) for i in range(dp_size)]
+
+    def ring_gather(block, turn, size, at):
+        parts = [block] + [lax.ppermute(block, "dp", turn(d)) for d in range(1, size)]
+        stacked = jnp.stack(parts[::-1] + parts[:0:-1])
+        return lax.dynamic_slice_in_dim(stacked, size - 1 - at, size, 0)
+
+    weight_row = ring_gather(crossed, x_turn, x_size, x_at)
+    weight_block = ring_gather(weight_row, z_turn, z_size, z_at).reshape(
+        dp_size * rows_dev, weight_rows.shape[1]
+    )
+    own_cols = jnp.concatenate(
+        [head_cols(weight_block, core, 128), head_cols(weight_block, 2 + core, 128)], axis=1
+    )
+    other_cols = jnp.concatenate(
+        [head_cols(weight_block, 1 - core, 128), head_cols(weight_block, 3 - core, 128)], axis=1
+    )
 
     tokens = activations.shape[0]
     piece = activations.shape[1] // (dp_size * seq_size)
@@ -330,6 +356,9 @@
         jnp.concatenate([dq_back, dq_own], axis=1),
     )
 
+    dkv_halo, dkv_own, act_all, own_cols, other_cols = lax.optimization_barrier(
+        (dkv_halo, dkv_own, act_all, own_cols, other_cols)
+    )
     kv_sum = dkv_own
     for d in range(1, halo_chips + 1):
         part = lax.ppermute(
@@ -345,21 +374,27 @@
         axis_index_groups=same_core,
     ).reshape(chips * 256, 256)
     kv_swap = lax.ppermute(kv_group, "seq", swap_cores)
-    low = jnp.where(core == 0, kv_group, kv_swap)
-    high = jnp.where(core == 0, kv_swap, kv_group)
-    kv_grad = jnp.concatenate(
-        [low[:, :128], high[:, :128], low[:, 128:], high[:, 128:]], axis=1
-    )
-
-    weight_part = dot(act_all, kv_grad, NN).astype(bf16)
-    got = lax.all_to_all(
-        weight_part.reshape(dp_size, piece, weight_part.shape[1]),
-        "dp",
-        split_axis=0,
-        concat_axis=0,
-    )
-    grad_weights = jnp.sum(got.astype(f32), axis=0)
-    grad_x_cols = dot(kv_grad, weight_block, NT).astype(bf16)
+    grad_x_cols = (dot(kv_group, own_cols, NT) + dot(kv_swap, other_cols, NT)).astype(bf16)
+    weight_part = jnp.concatenate(
+        [dot(act_all, kv_group, NN), dot(act_all, kv_swap, NN)], axis=1
+    ).astype(bf16)
+
+    def ring_scatter(blocks, turn, size, at):
+        total = lax.dynamic_index_in_dim(blocks, at, 0, keepdims=False).astype(f32)
+        for d in range(1, size):
+            block = lax.dynamic_index_in_dim(blocks, (at + d) % size, 0, keepdims=False)
+            total = total + lax.ppermute(block.astype(bf16), "dp", turn(d)).astype(f32)
+        return total
+
+    blocks = weight_part.reshape(z_size, x_size, piece, weight_part.shape[1]).transpose(1, 0, 2, 3)
+    in_row = ring_scatter(blocks, x_turn, x_size, x_at)
+    total = ring_scatter(in_row, z_turn, z_size, z_at)
+    own_k, own_v, other_k, other_v = (total[:, i * 128 : (i + 1) * 128] for i in range(4))
+    grad_weights = jnp.where(
+        core == 0,
+        jnp.concatenate([own_k, other_k, own_v, other_v], axis=1),
+        jnp.concatenate([other_k, own_k, other_v, own_v], axis=1),
+    )
     grad_x = lax.all_to_all(grad_x_cols, "seq", split_axis=0, concat_axis=1, tiled=True)
     return (grad_q, grad_x, grad_weights)
 

time: 204 us -> 177 us (0.87); the launches traced: 200 us -> 176 us
  blocking collectives: 45.6 us -> 18.8 us
  waiting for transfers between devices: 42.5 us -> 22.4 us
  local copies, waits for them, and re-layouts: 15.1 us -> 24.5 us
  starting transfers between devices: 56.5 us -> 64.8 us
  matrix products: 3.33 us -> 7.44 us
    all_gather x1 -> x0, blocking collectives: 45.6 us -> none  [on_device(): weight_block = lax.all_gather(crossed, 'dp', axis=0, tiled=True)]
    ppermute x0 -> x12, starting transfers between devices: none -> 22.2 us  [the longest x6 12.6 us: ring_gather(): lax.ppermute(block, 'dp', turn(d))]
    all_to_all x0 -> x1, blocking collectives: none -> 18.8 us  [on_device(): lax.all_to_all(jnp.broadcast_to(kv_chip[None], (chips,) + kv_chip.shape),...]
    all_to_all x2 -> x0, starting transfers between devices: 18.8 us -> none  [the longest x1 11.8 us: on_device(): lax.all_to_all(weight_part.reshape(dp_size, piece, weight_part.shape[1]),...]
    ppermute x0 -> x12, waiting for transfers between devices: none -> 10.2 us  [the longest x6 7.28 us: ring_scatter(): total = total + lax.ppermute(block.astype(bf16), 'dp', turn(d)).astype(f32)]
    all_to_all x1, waiting for transfers between devices: 10.2 us -> 0.01 us  [on_device(): lax.all_to_all(grad_x_cols, 'seq', split_axis=0, concat_axis=1, tiled=True)]
    all_to_all x2 -> x0, waiting for transfers between devices: 9.69 us -> none  [the longest x1 9.69 us: on_device(): lax.all_to_all(jnp.broadcast_to(kv_chip[None], (chips,) + kv_chip.shape),...]
    all_to_all x1, waiting for transfers between devices: 8.89 us -> 0.01 us  [on_device(): act_all = lax.all_to_all(act_rows, 'seq', split_axis=0, concat_axis=0)]
  transfers between devices with their start and end apart: 18 -> 28, of which waited for: 9 -> 8; matrix products, arithmetic and copies ran while one was open for 8% -> 15% of each run, Pallas kernels for 0% -> 18%
where the time goes in v2:
time: 177 us; the launch traced here: 176 us
  starting transfers between devices  64.8 us (37%)
  Pallas kernels  31.1 us (18%)
  local copies, waits for them, and re-layouts  24.5 us (14%)
  waiting for transfers between devices  22.4 us (13%)
  blocking collectives  18.8 us (11%)
  matrix products  7.44 us (4%)
  other arithmetic  6.09 us (3%)
    pallas_call x1, Pallas kernels, attend_grads(): pl.pallas_call(attention_kernel, grid_spec=pltpu.PrefetchScalarGridSpec(n...  31.1 us
    all_to_all x1, blocking collectives, on_device(): lax.all_to_all(jnp.broadcast_to(kv_chip[None], (chips,) + kv_chip.shape),...  18.8 us
    ppermute x4, starting transfers between devices, on_device(): lax.ppermute(kv_own, 'seq', [(i, i + 2 * d) for i in range(seq_size - 2 *...  12.9 us
    ppermute x6, starting transfers between devices, ring_gather(): lax.ppermute(block, 'dp', turn(d))  12.6 us
    unnamed x33, local copies, waits for them, and re-layouts  10.5 us
    ppermute x6, starting transfers between devices, ring_scatter(): total = total + lax.ppermute(block.astype(bf16), 'dp', turn(d)).astype(f32)  9.63 us
    ppermute x4, waiting for transfers between devices, on_device(): lax.ppermute(dkv_halo[halo_chips - d], 'seq', [(i, i - 2 * d) for i in ra...  9.61 us
    all_to_all x1, starting transfers between devices, on_device(): act_all = lax.all_to_all(act_rows, 'seq', split_axis=0, concat_axis=0)  9.05 us
  transfers between devices with their start and end apart: 28, of which 8 were waited for; matrix products, arithmetic and copies ran while one was open for 15% of the time, Pallas kernels for 18%

profile of v2, /device:TPU:8, one launch (start us, length us, event | category | flops | bytes accessed | tf_op | source)
XLA Modules:
  0.0 176.2 jit_solution(10014237940657931879)
XLA Ops:
  0.7 0.9 fusion.35
  1.7 0.8 fusion.18
  2.5 5.1 %collective-permute-start.8 = (bf16[16,512]{1,0:T(8,128)(2,1)S(1)}, bf16[16,512]{1,0:T(8,128)(2,1)S(1)}, u32[]{:S(2)}, u32[]{:S(2)}) collective-permute-start(bf16[16,512]{1,0:T(8,128)(2,1)S(1)} %fusion.18), channel_id=1, source_target_pairs={{0,0},{1,16},{2,32},{3,48},{4,64},{5,80},{6,96},{7,112},{8,128},{9... | collective-permute-start | bytes 49160 | tf_op jit(solution)/shard_map/ppermute | solution.py:300
  7.6 0.8 constant_dynamic-slice_fusion.10
  8.5 1.1 collective-permute-start.2
  9.6 1.9 %constant_dynamic-slice_fusion.12 = bf16[128,2048]{1,0:T(8,128)(2,1)} fusion(bf16[128,4096]{1,0:T(8,128)(2,1)} %g_own.1, s32[]{:T(128)S(6)} %select_n.164), kind=kLoop, calls=%fused_computation.107 | loop fusion | bytes 1048580 | tf_op jit(solution)/shard_map/dynamic_slice | solution.py:257
  11.6 0.8 pad_dynamic-slice_fusion.8
  12.6 0.8 constant_dynamic-slice_fusion.13
  13.4 0.7 constant_dynamic-slice_fusion.7
  14.1 3.5 %collective-permute-start.9 = (bf16[16,512]{1,0:T(8,128)(2,1)S(1)}, bf16[16,512]{1,0:T(8,128)(2,1)S(1)}, u32[]{:S(2)}, u32[]{:S(2)}) collective-permute-start(bf16[16,512]{1,0:T(8,128)(2,1)S(1)} %collective-permute-done.8), channel_id=1, source_target_pairs={{0,48},{16,0},{32,16},{48,32},{64,112},{80,64},{96,80},{112,96},{1... | collective-permute-start | bytes 49160 | tf_op jit(solution)/shard_map/ppermute | solution.py:322
  17.8 1.6 copy.23
  19.4 1.2 copy.24
  20.7 2.3 %collective-permute-start.10 = (bf16[16,512]{1,0:T(8,128)(2,1)S(1)}, bf16[16,512]{1,0:T(8,128)(2,1)S(1)}, u32[]{:S(2)}, u32[]{:S(2)}) collective-permute-start(bf16[16,512]{1,0:T(8,128)(2,1)S(1)} %collective-permute-done.8), channel_id=1, source_target_pairs={{0,32},{16,48},{32,0},{48,16},{64,96},{80,112},{96,64},{112,80},{1... | collective-permute-start | bytes 49160 | tf_op jit(solution)/shard_map/ppermute | solution.py:322
  23.0 2.9 %collective-permute-done.10 = bf16[16,512]{1,0:T(8,128)(2,1)S(1)} collective-permute-done((bf16[16,512]{1,0:T(8,128)(2,1)S(1)}, bf16[16,512]{1,0:T(8,128)(2,1)S(1)}, u32[]{:S(2)}, u32[]{:S(2)}) %collective-permute-start.10) | collective-permute-done | bytes 16416 | tf_op jit(solution)/shard_map/ppermute | solution.py:322
  26.0 0.6 constant_dynamic-slice_fusion.5
  26.6 4.2 %collective-permute-start.13 = (bf16[4,16,512]{2,1,0:T(8,128)(2,1)}, bf16[4,16,512]{2,1,0:T(8,128)(2,1)S(1)}, u32[]{:S(2)}, u32[]{:S(2)}) collective-permute-start(bf16[4,16,512]{2,1,0:T(8,128)(2,1)} %constant_dynamic-slice_fusion.5), channel_id=1, source_target_pairs={{0,128},{16,144},{32,160},{48,176},{64,192},{80,208},{96,224},{112... | collective-permute-start | bytes 196616 | tf_op jit(solution)/shard_map/ppermute | solution.py:322
  30.8 2.4 %collective-permute-start.12 = (bf16[4,16,512]{2,1,0:T(8,128)(2,1)}, bf16[4,16,512]{2,1,0:T(8,128)(2,1)S(1)}, u32[]{:S(2)}, u32[]{:S(2)}) collective-permute-start(bf16[4,16,512]{2,1,0:T(8,128)(2,1)} %constant_dynamic-slice_fusion.5), channel_id=1, source_target_pairs={{0,192},{16,208},{32,224},{48,240},{64,0},{80,16},{96,32},{112,48}... | collective-permute-start | bytes 196616 | tf_op jit(solution)/shard_map/ppermute | solution.py:322
  33.2 0.6 copy-done.9
  33.9 0.9 maximum_select_fusion.1.kv_own
  34.8 3.0 %collective-permute-start.6 = (bf16[256,256]{1,0:T(8,128)(2,1)S(1)}, bf16[256,256]{1,0:T(8,128)(2,1)S(1)}, u32[]{:S(2)}, u32[]{:S(2)}) collective-permute-start(bf16[256,256]{1,0:T(8,128)(2,1)S(1)} %maximum_select_fusion.1.kv_own), channel_id=1, source_target_pairs={{0,2},{1,3},{2,4},{3,5},{4,6},{5,7},{6,8},{7,9},{8,10},{9,11},{10,... | collective-permute-start | bytes 393224 | tf_op jit(solution)/shard_map/ppermute | solution.py:273
  37.8 4.9 %collective-permute-start.5 = (bf16[256,256]{1,0:T(8,128)(2,1)S(1)}, bf16[256,256]{1,0:T(8,128)(2,1)S(1)}, u32[]{:S(2)}, u32[]{:S(2)}) collective-permute-start(bf16[256,256]{1,0:T(8,128)(2,1)S(1)} %maximum_select_fusion.1.kv_own), channel_id=1, source_target_pairs={{0,4},{1,5},{2,6},{3,7},{4,8},{5,9},{6,10},{7,11},{8,12},{9,13},{1... | collective-permute-start | bytes 393224 | tf_op jit(solution)/shard_map/ppermute | solution.py:273
  42.7 3.7 %collective-permute-start.4 = (bf16[256,256]{1,0:T(8,128)(2,1)S(1)}, bf16[256,256]{1,0:T(8,128)(2,1)S(1)}, u32[]{:S(2)}, u32[]{:S(2)}) collective-permute-start(bf16[256,256]{1,0:T(8,128)(2,1)S(1)} %maximum_select_fusion.1.kv_own), channel_id=1, source_target_pairs={{0,6},{1,7},{2,8},{3,9},{4,10},{5,11},{6,12},{7,13},{8,14},{9,15},... | collective-permute-start | bytes 393224 | tf_op jit(solution)/shard_map/ppermute | solution.py:273
  46.4 0.6 bitcast_dynamic-update-slice_fusion.5
  47.0 1.3 collective-permute-start.3
  48.3 0.6 bitcast_dynamic-update-slice_fusion.3
  49.1 2.1 %collective-permute-done.3 = bf16[256,256]{1,0:T(8,128)(2,1)S(1)} collective-permute-done((bf16[256,256]{1,0:T(8,128)(2,1)S(1)}, bf16[256,256]{1,0:T(8,128)(2,1)S(1)}, u32[]{:S(2)}, u32[]{:S(2)}) %collective-permute-start.3) | collective-permute-done | bytes 131104 | tf_op jit(solution)/shard_map/ppermute | solution.py:273
  51.2 9.0 %all-to-all-start = ((bf16[16,256,128]{2,1,0:T(8,128)(2,1)}), bf16[16,256,128]{2,1,0:T(8,128)(2,1)}, u32[]{:S(2)}, u32[]{:S(2)}) async-start(bf16[16,256,128]{2,1,0:T(8,128)(2,1)} %bitcast.95), calls=%async_computation | async-start | bytes 2097152 | tf_op jit(solution)/shard_map/all_to_all | solution.py:345
  60.3 0.6 bitcast_dynamic-update-slice_fusion.1
  60.9 0.6 bitcast_dynamic-update-slice_fusion
  61.6 0.6 bitcast_dynamic-update-slice_fusion.6
  62.2 0.6 bitcast_dynamic-update-slice_fusion.4
  62.8 0.6 bitcast_dynamic-update-slice_fusion.2
  63.5 1.0 constant_dynamic-slice_fusion.4
  64.5 0.7 pad_maximum_fusion.1
  65.2 0.8 copy-done.4
  66.0 0.8 copy-done.6
  66.8 1.0 copy-done.5
  67.9 1.0 copy-done.7
  68.9 31.1 %shard_map.103 = (bf16[128,2048]{1,0:T(8,128)(2,1)S(1)}, bf16[128,2048]{1,0:T(8,128)(2,1)S(1)}, bf16[4,256,256]{2,1,0:T(8,128)(2,1)S(1)}, f32[256,256]{1,0:T(8,128)S(1)}) custom-call(s32[1]{0:T(128)} %bitcast.core_ref, bf16[128,4096]{1,0:T(8,128)(2,1)S(1)} %copy-done, bf16[128,4096]{1,0:T(8,128)(2,1)S(1)} %copy-done.1, bf16[128,2048]{1,0:T(8,128)(2,1)S(1)} %copy-done.7, ...), custom_call_target="tpu_custom_call" | custom-call | flops 7247757312 | bytes 5242880 | tf_op jit(solution)/shard_map/pallas_call | solution.py:184
  100.0 0.8 copy-done.2
  100.8 1.5 copy.25
  102.4 3.4 %collective-permute-start.15 = (bf16[256,256]{1,0:T(8,128)(2,1)S(1)}, bf16[256,256]{1,0:T(8,128)(2,1)S(1)}, u32[]{:S(2)}, u32[]{:S(2)}) collective-permute-start(bf16[256,256]{1,0:T(8,128)(2,1)S(1)} %get-tuple-element.23), channel_id=1, source_target_pairs={{2,0},{3,1},{4,2},{5,3},{6,4},{7,5},{8,6},{9,7},{10,8},{11,9},{12,... | collective-permute-start | bytes 393224 | tf_op jit(solution)/shard_map/ppermute | solution.py:364
  105.7 1.3 collective-permute-start.18
  107.0 1.3 collective-permute-start.17
  108.3 2.1 %collective-permute-start.16 = (bf16[256,256]{1,0:T(8,128)(2,1)S(1)}, bf16[256,256]{1,0:T(8,128)(2,1)S(1)}, u32[]{:S(2)}, u32[]{:S(2)}) collective-permute-start(bf16[256,256]{1,0:T(8,128)(2,1)S(1)} %get-tuple-element.26), channel_id=1, source_target_pairs={{4,0},{5,1},{6,2},{7,3},{8,4},{9,5},{10,6},{11,7},{12,8},{13,9},{1... | collective-permute-start | bytes 393224 | tf_op jit(solution)/shard_map/ppermute | solution.py:364
  110.4 7.9 %collective-permute-done.18 = bf16[256,256]{1,0:T(8,128)(2,1)S(1)} collective-permute-done((bf16[256,256]{1,0:T(8,128)(2,1)S(1)}, bf16[256,256]{1,0:T(8,128)(2,1)S(1)}, u32[]{:S(2)}, u32[]{:S(2)}) %collective-permute-start.18) | collective-permute-done | bytes 131104 | tf_op jit(solution)/shard_map/ppermute | solution.py:364
  118.3 1.7 collective-permute-done.16
  120.2 18.8 %all_to_all.29 = bf16[8,256,256]{2,1,0:T(8,128)(2,1)S(1)} all-to-all(bf16[8,256,256]{2,1,0:T(8,128)(2,1)S(1)} %broadcast_in_dim.15), channel_id=1, replica_groups={{0,2,4,6,8,10,12,14},{1,3,5,7,9,11,13,15},{16,18,20,22,24,26,28,30},{17..., dimensions={0} | all-to-all | bytes 2097152 | tf_op jit(solution)/shard_map/all_to_all | solution.py:369
  139.0 0.5 collective-permute-start.7
  139.5 1.4 copy.28
  141.8 2.7 %fusion = bf16[2048,256]{1,0:T(8,128)(2,1)} fusion(f32[2048,256]{1,0:T(8,128)S(1)} %fusion.43, bf16[2048,256]{1,0:T(8,128)(2,1)} %collective-permute-done.19, bf16[256,256]{1,0:T(8,128)(2,1)S(1)} %get-tuple-element.21), kind=kOutput, calls=%fused_computation.1 | convolution fusion | flops 269484032 | bytes 4325376 | tf_op jit(solution)/shard_map/dot_general | solution.py:28
  144.5 6.0 %all-to-all-start.2 = ((bf16[16,128,256]{2,1,0:T(8,128)(2,1)}), bf16[16,128,256]{2,1,0:T(8,128)(2,1)}, u32[]{:S(2)}, u32[]{:S(2)}) async-start(bf16[16,128,256]{2,1,0:T(8,128)(2,1)} %bitcast.98), calls=%async_computation.2 | async-start | bytes 2097152 | tf_op jit(solution)/shard_map/all_to_all | solution.py:398
  150.4 1.7 convolution_convert_fusion.1
  152.1 1.7 convolution_convert_fusion
  154.0 3.1 %collective-permute-start.21 = (bf16[4,16,512]{2,1,0:T(8,128)(2,1)S(1)}, bf16[4,16,512]{2,1,0:T(8,128)(2,1)S(1)}, u32[]{:S(2)}, u32[]{:S(2)}) collective-permute-start(bf16[4,16,512]{2,1,0:T(8,128)(2,1)S(1)} %get-tuple-element.28), channel_id=1, source_target_pairs={{0,32},{16,48},{32,0},{48,16},{64,96},{80,112},{96,64},{112,80},{1... | collective-permute-start | bytes 196616 | tf_op jit(solution)/shard_map/ppermute | solution.py:386
  157.1 0.8 collective-permute-start.22
  157.8 2.9 %collective-permute-done.20 = bf16[4,16,512]{2,1,0:T(8,128)(2,1)S(1)} collective-permute-done((bf16[4,16,512]{2,1,0:T(8,128)(2,1)S(1)}, bf16[4,16,512]{2,1,0:T(8,128)(2,1)S(1)}, u32[]{:S(2)}, u32[]{:S(2)}) %collective-permute-start.20) | collective-permute-done | bytes 65568 | tf_op jit(solution)/shard_map/ppermute | solution.py:386
  160.7 0.6 collective-permute-done.22
  161.5 4.1 %collective-permute-start.25 = (bf16[16,512]{1,0:T(8,128)(2,1)S(1)}, bf16[16,512]{1,0:T(8,128)(2,1)S(1)}, u32[]{:S(2)}, u32[]{:S(2)}) collective-permute-start(bf16[16,512]{1,0:T(8,128)(2,1)S(1)} %get-tuple-element.35), channel_id=1, source_target_pairs={{0,192},{16,208},{32,224},{48,240},{64,0},{80,16},{96,32},{112,48}... | collective-permute-start | bytes 49160 | tf_op jit(solution)/shard_map/ppermute | solution.py:386
  165.6 1.5 collective-permute-start.24
  167.1 2.4 %maximum_select_fusion = bf16[128,4096]{1,0:T(8,128)(2,1)} fusion(bf16[128,2048]{1,0:T(8,128)(2,1)} %collective-permute-done.7, bf16[128,2048]{1,0:T(8,128)(2,1)S(1)} %get-tuple-element.13, pred[]{:T(512)S(6)} %eq.56), kind=kLoop, calls=%fused_computation.4 | loop fusion | flops 4718592 | bytes 2097153 | tf_op jit(solution)/shard_map/jit(_where)/select_n | solution.py:353
  169.5 3.8 %collective-permute-done.24 = bf16[16,512]{1,0:T(8,128)(2,1)S(1)} collective-permute-done((bf16[16,512]{1,0:T(8,128)(2,1)S(1)}, bf16[16,512]{1,0:T(8,128)(2,1)S(1)}, u32[]{:S(2)}, u32[]{:S(2)}) %collective-permute-start.24) | collective-permute-done | bytes 16416 | tf_op jit(solution)/shard_map/ppermute | solution.py:386
  173.3 0.6 maximum_select_fusion.2
  173.9 2.3 %copy.31 = bf16[16,16,8,256]{3,2,0,1:T(8,128)(2,1)} copy(bf16[16,16,8,256]{3,2,1,0:T(8,128)(2,1)} %bitcast.45) | data formatting | bytes 2097152 | tf_op jit(solution)/shard_map/all_to_all | solution.py:398
  (66 shorter events, 2.1 us)
Async XLA Ops:
  0.6 11.9 %copy-start = (bf16[128,4096]{1,0:T(8,128)(2,1)S(1)}, bf16[128,4096]{1,0:T(8,128)(2,1)}, u32[]{:S(2)}) copy-start(bf16[128,4096]{1,0:T(8,128)(2,1)} %q_own.1) | copy-start | bytes 3145732
  2.5 11.6 %collective-permute-start.8 = (bf16[16,512]{1,0:T(8,128)(2,1)S(1)}, bf16[16,512]{1,0:T(8,128)(2,1)S(1)}, u32[]{:S(2)}, u32[]{:S(2)}) collective-permute-start(bf16[16,512]{1,0:T(8,128)(2,1)S(1)} %fusion.18), channel_id=1, source_target_pairs={{0,0},{1,16},{2,32},{3,48},{4,64},{5,80},{6,96},{7,112},{8,128},{9... | collective-permute-start | bytes 49160 | tf_op jit(solution)/shard_map/ppermute | solution.py:300
  8.5 24.7 %collective-permute-start.2 = (bf16[128,256]{1,0:T(8,128)(2,1)S(1)}, bf16[128,256]{1,0:T(8,128)(2,1)S(1)}, u32[]{:S(2)}, u32[]{:S(2)}) collective-permute-start(bf16[128,256]{1,0:T(8,128)(2,1)S(1)} %pad_maximum_fusion.3), channel_id=1, source_target_pairs={{0,1},{1,0},{2,3},{3,2},{4,5},{5,4},{6,7},{7,6},{8,9},{9,8},{10,11... | collective-permute-start | bytes 196616 | tf_op jit(solution)/shard_map/ppermute | solution.py:265
  11.5 53.7 %collective-permute-start.1 = (bf16[128,2048]{1,0:T(8,128)(2,1)}, bf16[128,2048]{1,0:T(8,128)(2,1)S(1)}, u32[]{:S(2)}, u32[]{:S(2)}) collective-permute-start(bf16[128,2048]{1,0:T(8,128)(2,1)} %constant_dynamic-slice_fusion.12), channel_id=1, source_target_pairs={{0,1},{1,0},{2,3},{3,2},{4,5},{5,4},{6,7},{7,6},{8,9},{9,8},{10,11... | collective-permute-start | bytes 1572872 | tf_op jit(solution)/shard_map/ppermute | solution.py:278
  14.1 8.9 %collective-permute-start.9 = (bf16[16,512]{1,0:T(8,128)(2,1)S(1)}, bf16[16,512]{1,0:T(8,128)(2,1)S(1)}, u32[]{:S(2)}, u32[]{:S(2)}) collective-permute-start(bf16[16,512]{1,0:T(8,128)(2,1)S(1)} %collective-permute-done.8), channel_id=1, source_target_pairs={{0,48},{16,0},{32,16},{48,32},{64,112},{80,64},{96,80},{112,96},{1... | collective-permute-start | bytes 49160 | tf_op jit(solution)/shard_map/ppermute | solution.py:322
  20.7 5.3 %collective-permute-start.11 = (bf16[16,512]{1,0:T(8,128)(2,1)S(1)}, bf16[16,512]{1,0:T(8,128)(2,1)S(1)}, u32[]{:S(2)}, u32[]{:S(2)}) collective-permute-start(bf16[16,512]{1,0:T(8,128)(2,1)S(1)} %collective-permute-done.8), channel_id=1, source_target_pairs={{0,16},{16,32},{32,48},{48,0},{64,80},{80,96},{96,112},{112,64},{1... | collective-permute-start | bytes 49160 | tf_op jit(solution)/shard_map/ppermute | solution.py:322
  20.7 5.2 %collective-permute-start.10 = (bf16[16,512]{1,0:T(8,128)(2,1)S(1)}, bf16[16,512]{1,0:T(8,128)(2,1)S(1)}, u32[]{:S(2)}, u32[]{:S(2)}) collective-permute-start(bf16[16,512]{1,0:T(8,128)(2,1)S(1)} %collective-permute-done.8), channel_id=1, source_target_pairs={{0,32},{16,48},{32,0},{48,16},{64,96},{80,112},{96,64},{112,80},{1... | collective-permute-start | bytes 49160 | tf_op jit(solution)/shard_map/ppermute | solution.py:322
  26.6 20.4 %collective-permute-start.13 = (bf16[4,16,512]{2,1,0:T(8,128)(2,1)}, bf16[4,16,512]{2,1,0:T(8,128)(2,1)S(1)}, u32[]{:S(2)}, u32[]{:S(2)}) collective-permute-start(bf16[4,16,512]{2,1,0:T(8,128)(2,1)} %constant_dynamic-slice_fusion.5), channel_id=1, source_target_pairs={{0,128},{16,144},{32,160},{48,176},{64,192},{80,208},{96,224},{112... | collective-permute-start | bytes 196616 | tf_op jit(solution)/shard_map/ppermute | solution.py:322
  30.8 11.9 %collective-permute-start.12 = (bf16[4,16,512]{2,1,0:T(8,128)(2,1)}, bf16[4,16,512]{2,1,0:T(8,128)(2,1)S(1)}, u32[]{:S(2)}, u32[]{:S(2)}) collective-permute-start(bf16[4,16,512]{2,1,0:T(8,128)(2,1)} %constant_dynamic-slice_fusion.5), channel_id=1, source_target_pairs={{0,192},{16,208},{32,224},{48,240},{64,0},{80,16},{96,32},{112,48}... | collective-permute-start | bytes 196616 | tf_op jit(solution)/shard_map/ppermute | solution.py:322
  33.2 0.6 copy-start.9
  34.8 14.2 %collective-permute-start.6 = (bf16[256,256]{1,0:T(8,128)(2,1)S(1)}, bf16[256,256]{1,0:T(8,128)(2,1)S(1)}, u32[]{:S(2)}, u32[]{:S(2)}) collective-permute-start(bf16[256,256]{1,0:T(8,128)(2,1)S(1)} %maximum_select_fusion.1.kv_own), channel_id=1, source_target_pairs={{0,2},{1,3},{2,4},{3,5},{4,6},{5,7},{6,8},{7,9},{8,10},{9,11},{10,... | collective-permute-start | bytes 393224 | tf_op jit(solution)/shard_map/ppermute | solution.py:273
  37.8 11.2 %collective-permute-start.5 = (bf16[256,256]{1,0:T(8,128)(2,1)S(1)}, bf16[256,256]{1,0:T(8,128)(2,1)S(1)}, u32[]{:S(2)}, u32[]{:S(2)}) collective-permute-start(bf16[256,256]{1,0:T(8,128)(2,1)S(1)} %maximum_select_fusion.1.kv_own), channel_id=1, source_target_pairs={{0,4},{1,5},{2,6},{3,7},{4,8},{5,9},{6,10},{7,11},{8,12},{9,13},{1... | collective-permute-start | bytes 393224 | tf_op jit(solution)/shard_map/ppermute | solution.py:273
  42.7 6.4 %collective-permute-start.4 = (bf16[256,256]{1,0:T(8,128)(2,1)S(1)}, bf16[256,256]{1,0:T(8,128)(2,1)S(1)}, u32[]{:S(2)}, u32[]{:S(2)}) collective-permute-start(bf16[256,256]{1,0:T(8,128)(2,1)S(1)} %maximum_select_fusion.1.kv_own), channel_id=1, source_target_pairs={{0,6},{1,7},{2,8},{3,9},{4,10},{5,11},{6,12},{7,13},{8,14},{9,15},... | collective-permute-start | bytes 393224 | tf_op jit(solution)/shard_map/ppermute | solution.py:273
  47.0 4.1 %collective-permute-start.3 = (bf16[256,256]{1,0:T(8,128)(2,1)S(1)}, bf16[256,256]{1,0:T(8,128)(2,1)S(1)}, u32[]{:S(2)}, u32[]{:S(2)}) collective-permute-start(bf16[256,256]{1,0:T(8,128)(2,1)S(1)} %maximum_select_fusion.1.kv_own), channel_id=1, source_target_pairs={{0,8},{1,9},{2,10},{3,11},{4,12},{5,13},{6,14},{7,15},{16,24},{17,... | collective-permute-start | bytes 393224 | tf_op jit(solution)/shard_map/ppermute | solution.py:273
  49.0 17.1 %collective-permute-start = (bf16[128,2048]{1,0:T(8,128)(2,1)}, bf16[128,2048]{1,0:T(8,128)(2,1)S(1)}, u32[]{:S(2)}, u32[]{:S(2)}) collective-permute-start(bf16[128,2048]{1,0:T(8,128)(2,1)} %constant_dynamic-slice_fusion.13), channel_id=1, source_target_pairs={{0,1},{1,0},{2,3},{3,2},{4,5},{5,4},{6,7},{7,6},{8,9},{9,8},{10,11... | collective-permute-start | bytes 1572872 | tf_op jit(solution)/shard_map/ppermute | solution.py:277
  49.0 11.3 %collective-permute-start.14 = (bf16[4,16,512]{2,1,0:T(8,128)(2,1)}, bf16[4,16,512]{2,1,0:T(8,128)(2,1)S(1)}, u32[]{:S(2)}, u32[]{:S(2)}) collective-permute-start(bf16[4,16,512]{2,1,0:T(8,128)(2,1)} %constant_dynamic-slice_fusion.5), channel_id=1, source_target_pairs={{0,64},{16,80},{32,96},{48,112},{64,128},{80,144},{96,160},{112,17... | collective-permute-start | bytes 196616 | tf_op jit(solution)/shard_map/ppermute | solution.py:322
  51.2 49.6 %all-to-all-start = ((bf16[16,256,128]{2,1,0:T(8,128)(2,1)}), bf16[16,256,128]{2,1,0:T(8,128)(2,1)}, u32[]{:S(2)}, u32[]{:S(2)}) async-start(bf16[16,256,128]{2,1,0:T(8,128)(2,1)} %bitcast.95), calls=%async_computation | async-start | bytes 2097152 | tf_op jit(solution)/shard_map/all_to_all | solution.py:345
  60.3 6.5 %copy-start.1 = (bf16[128,4096]{1,0:T(8,128)(2,1)S(1)}, bf16[128,4096]{1,0:T(8,128)(2,1)}, u32[]{:S(2)}) copy-start(bf16[128,4096]{1,0:T(8,128)(2,1)} %g_own.1) | copy-start | bytes 3145732
  65.2 0.8 copy-start.4
  66.0 0.8 copy-start.6
  66.8 1.0 copy-start.5
  67.9 1.0 copy-start.7
  100.0 0.8 copy-start.2
  102.4 8.1 %collective-permute-start.15 = (bf16[256,256]{1,0:T(8,128)(2,1)S(1)}, bf16[256,256]{1,0:T(8,128)(2,1)S(1)}, u32[]{:S(2)}, u32[]{:S(2)}) collective-permute-start(bf16[256,256]{1,0:T(8,128)(2,1)S(1)} %get-tuple-element.23), channel_id=1, source_target_pairs={{2,0},{3,1},{4,2},{5,3},{6,4},{7,5},{8,6},{9,7},{10,8},{11,9},{12,... | collective-permute-start | bytes 393224 | tf_op jit(solution)/shard_map/ppermute | solution.py:364
  105.7 12.6 %collective-permute-start.18 = (bf16[256,256]{1,0:T(8,128)(2,1)S(1)}, bf16[256,256]{1,0:T(8,128)(2,1)S(1)}, u32[]{:S(2)}, u32[]{:S(2)}) collective-permute-start(bf16[256,256]{1,0:T(8,128)(2,1)S(1)} %get-tuple-element.24), channel_id=1, source_target_pairs={{8,0},{9,1},{10,2},{11,3},{12,4},{13,5},{14,6},{15,7},{24,16},{25,... | collective-permute-start | bytes 393224 | tf_op jit(solution)/shard_map/ppermute | solution.py:364
  107.0 11.3 %collective-permute-start.17 = (bf16[256,256]{1,0:T(8,128)(2,1)S(1)}, bf16[256,256]{1,0:T(8,128)(2,1)S(1)}, u32[]{:S(2)}, u32[]{:S(2)}) collective-permute-start(bf16[256,256]{1,0:T(8,128)(2,1)S(1)} %get-tuple-element.25), channel_id=1, source_target_pairs={{6,0},{7,1},{8,2},{9,3},{10,4},{11,5},{12,6},{13,7},{14,8},{15,9},... | collective-permute-start | bytes 393224 | tf_op jit(solution)/shard_map/ppermute | solution.py:364
  108.3 30.7 %copy-start.3 = (bf16[128,2048]{1,0:T(8,128)(2,1)S(1)}, bf16[128,2048]{1,0:T(8,128)(2,1)}, u32[]{:S(2)}) copy-start(bf16[128,2048]{1,0:T(8,128)(2,1)} %copy-done.2) | copy-start | bytes 1572868
  108.3 11.7 %collective-permute-start.16 = (bf16[256,256]{1,0:T(8,128)(2,1)S(1)}, bf16[256,256]{1,0:T(8,128)(2,1)S(1)}, u32[]{:S(2)}, u32[]{:S(2)}) collective-permute-start(bf16[256,256]{1,0:T(8,128)(2,1)S(1)} %get-tuple-element.26), channel_id=1, source_target_pairs={{4,0},{5,1},{6,2},{7,3},{8,4},{9,5},{10,6},{11,7},{12,8},{13,9},{1... | collective-permute-start | bytes 393224 | tf_op jit(solution)/shard_map/ppermute | solution.py:364
  120.2 20.8 %copy-start.8 = (bf16[256,256]{1,0:T(8,128)(2,1)S(1)}, bf16[256,256]{1,0:T(8,128)(2,1)}, u32[]{:S(2)}) copy-start(bf16[256,256]{1,0:T(8,128)(2,1)} %get-tuple-element.20) | copy-start | bytes 393220
  139.0 2.8 %collective-permute-start.19 = (bf16[2048,256]{1,0:T(8,128)(2,1)S(1)}, bf16[2048,256]{1,0:T(8,128)(2,1)}, u32[]{:S(2)}, u32[]{:S(2)}) collective-permute-start(bf16[2048,256]{1,0:T(8,128)(2,1)S(1)} %bitcast.90), channel_id=1, source_target_pairs={{0,1},{1,0},{2,3},{3,2},{4,5},{5,4},{6,7},{7,6},{8,9},{9,8},{10,11... | collective-permute-start | bytes 3145736 | tf_op jit(solution)/shard_map/ppermute | solution.py:376
  139.0 28.0 %collective-permute-start.7 = (bf16[128,2048]{1,0:T(8,128)(2,1)S(1)}, bf16[128,2048]{1,0:T(8,128)(2,1)}, u32[]{:S(2)}, u32[]{:S(2)}) collective-permute-start(bf16[128,2048]{1,0:T(8,128)(2,1)S(1)} %copy-done.3), channel_id=1, source_target_pairs={{0,1},{1,0},{2,3},{3,2},{4,5},{5,4},{6,7},{7,6},{8,9},{9,8},{10,11... | collective-permute-start | bytes 1572872 | tf_op jit(solution)/shard_map/ppermute | solution.py:352
  144.5 29.4 %all-to-all-start.2 = ((bf16[16,128,256]{2,1,0:T(8,128)(2,1)}), bf16[16,128,256]{2,1,0:T(8,128)(2,1)}, u32[]{:S(2)}, u32[]{:S(2)}) async-start(bf16[16,128,256]{2,1,0:T(8,128)(2,1)} %bitcast.98), calls=%async_computation.2 | async-start | bytes 2097152 | tf_op jit(solution)/shard_map/all_to_all | solution.py:398
  153.9 6.8 %collective-permute-start.20 = (bf16[4,16,512]{2,1,0:T(8,128)(2,1)S(1)}, bf16[4,16,512]{2,1,0:T(8,128)(2,1)S(1)}, u32[]{:S(2)}, u32[]{:S(2)}) collective-permute-start(bf16[4,16,512]{2,1,0:T(8,128)(2,1)S(1)} %get-tuple-element.27), channel_id=1, source_target_pairs={{0,16},{16,32},{32,48},{48,0},{64,80},{80,96},{96,112},{112,64},{1... | collective-permute-start | bytes 196616 | tf_op jit(solution)/shard_map/ppermute | solution.py:386
  154.0 6.8 %collective-permute-start.21 = (bf16[4,16,512]{2,1,0:T(8,128)(2,1)S(1)}, bf16[4,16,512]{2,1,0:T(8,128)(2,1)S(1)}, u32[]{:S(2)}, u32[]{:S(2)}) collective-permute-start(bf16[4,16,512]{2,1,0:T(8,128)(2,1)S(1)} %get-tuple-element.28), channel_id=1, source_target_pairs={{0,32},{16,48},{32,0},{48,16},{64,96},{80,112},{96,64},{112,80},{1... | collective-permute-start | bytes 196616 | tf_op jit(solution)/shard_map/ppermute | solution.py:386
  157.1 4.3 %collective-permute-start.22 = (bf16[4,16,512]{2,1,0:T(8,128)(2,1)S(1)}, bf16[4,16,512]{2,1,0:T(8,128)(2,1)S(1)}, u32[]{:S(2)}, u32[]{:S(2)}) collective-permute-start(bf16[4,16,512]{2,1,0:T(8,128)(2,1)S(1)} %get-tuple-element.29), channel_id=1, source_target_pairs={{0,48},{16,0},{32,16},{48,32},{64,112},{80,64},{96,80},{112,96},{1... | collective-permute-start | bytes 196616 | tf_op jit(solution)/shard_map/ppermute | solution.py:386
  161.4 8.1 %collective-permute-start.23 = (bf16[16,512]{1,0:T(8,128)(2,1)S(1)}, bf16[16,512]{1,0:T(8,128)(2,1)S(1)}, u32[]{:S(2)}, u32[]{:S(2)}) collective-permute-start(bf16[16,512]{1,0:T(8,128)(2,1)S(1)} %get-tuple-element.34), channel_id=1, source_target_pairs={{0,64},{16,80},{32,96},{48,112},{64,128},{80,144},{96,160},{112,17... | collective-permute-start | bytes 49160 | tf_op jit(solution)/shard_map/ppermute | solution.py:386
  161.5 8.0 %collective-permute-start.25 = (bf16[16,512]{1,0:T(8,128)(2,1)S(1)}, bf16[16,512]{1,0:T(8,128)(2,1)S(1)}, u32[]{:S(2)}, u32[]{:S(2)}) collective-permute-start(bf16[16,512]{1,0:T(8,128)(2,1)S(1)} %get-tuple-element.35), channel_id=1, source_target_pairs={{0,192},{16,208},{32,224},{48,240},{64,0},{80,16},{96,32},{112,48}... | collective-permute-start | bytes 49160 | tf_op jit(solution)/shard_map/ppermute | solution.py:386
  165.6 7.6 %collective-permute-start.24 = (bf16[16,512]{1,0:T(8,128)(2,1)S(1)}, bf16[16,512]{1,0:T(8,128)(2,1)S(1)}, u32[]{:S(2)}, u32[]{:S(2)}) collective-permute-start(bf16[16,512]{1,0:T(8,128)(2,1)S(1)} %get-tuple-element.36), channel_id=1, source_target_pairs={{0,128},{16,144},{32,160},{48,176},{64,192},{80,208},{96,224},{112... | collective-permute-start | bytes 49160 | tf_op jit(solution)/shard_map/ppermute | solution.py:386

commit v3 on v2

--- a/solution.py
+++ b/solution.py
@@ -14,7 +14,9 @@
 GROUP_HEADS = QUERY_HEADS // KEY_VALUE_HEADS
 GROUP_COLS = GROUP_HEADS * HEAD_WIDTH
 DOC_LIMIT = 1024
-HEADS_STEP = 4
+HEADS_STEP = 8
+WIDEN = 4
+ROW_TILE = 256
 
 masked_bias = -1e30
 score_scale = 1.0 / math.sqrt(HEAD_WIDTH)
@@ -43,12 +45,18 @@
     q_other,
     g_other,
     kv_own,
-    kv_halo,
+    kv_1,
+    kv_2,
+    kv_3,
+    kv_4,
     key_mark,
     query_mark,
     dq_own,
     dq_other,
-    dkv_halo,
+    dkv_1,
+    dkv_2,
+    dkv_3,
+    dkv_4,
     dkv_own,
     ka,
     kt,
@@ -71,8 +79,7 @@
     @pl.when((slot == 0) & (step == 0))
     def _():
         ka[:, 128:] = key_mark[...]
-        for i in range(DOC_LIMIT // 256 + 1):
-            block = kv_halo[i] if i < DOC_LIMIT // 256 else kv_own[...]
+        for i, block in enumerate((kv_4, kv_3, kv_2, kv_1, kv_own)):
             at = slice(i * 256, (i + 1) * 256)
             ka[at, :128] = block[:, :128]
             va[at, :] = block[:, 128:]
@@ -99,44 +106,41 @@
 
     half = (core_ref[0] + slot) % 2
     first = pl.multiple_of(half * 128, 128)
-    q_all = qa[...]
-    g_all = ga[...]
-
-    best = jnp.full((8, rows), masked_bias, jnp.float32)
-    for b in range(blocks):
-        at = pl.ds(pl.multiple_of(first + b * 128, 128), 128)
-        s = dot(ka[at, :], q_all, NT)
-        if b == blocks - 1:
-            key_at = lax.broadcasted_iota(jnp.int32, (128, rows), 0)
-            query_at = lax.broadcasted_iota(jnp.int32, (128, rows), 1) % 128
-            s = jnp.where(key_at <= query_at, s, masked_bias)
-        s_scr[b * 128 : (b + 1) * 128, :] = s
-        best = jnp.maximum(best, jnp.max(s.reshape(16, 8, rows), axis=0))
-        d_scr[b * 128 : (b + 1) * 128, :] = dot(va[at, :], g_all, NT)
-    row_max = jnp.max(best, axis=0, keepdims=True) * exp2_scale
-    total = jnp.zeros((8, rows), jnp.float32)
-    for b in range(blocks):
-        here = slice(b * 128, (b + 1) * 128)
-        e = jnp.exp2(s_scr[here, :] * exp2_scale - row_max)
-        s_scr[here, :] = e
-        total = total + jnp.sum(e.reshape(16, 8, rows), axis=0)
-    inverse = 1.0 / jnp.sum(total, axis=0, keepdims=True)
-    delta = jnp.zeros((8, rows), jnp.float32)
-    for b in range(blocks):
-        here = slice(b * 128, (b + 1) * 128)
-        p = s_scr[here, :] * inverse
-        s_scr[here, :] = p
-        p_bf = p.astype(jnp.bfloat16)
-        p_scr[here, :] = p_bf
-        term = p_bf.astype(jnp.float32) * d_scr[here, :]
-        delta = delta + jnp.sum(term.reshape(16, 8, rows), axis=0)
-    row_delta = jnp.sum(delta, axis=0, keepdims=True)
-    for b in range(blocks):
-        here = slice(b * 128, (b + 1) * 128)
-        ds_scr[here, :] = (s_scr[here, :] * (d_scr[here, :] - row_delta)).astype(jnp.bfloat16)
+    for t in range(rows // ROW_TILE):
+        lanes = slice(t * ROW_TILE, (t + 1) * ROW_TILE)
+        q_tile = qa[lanes, :]
+        g_tile = ga[lanes, :]
+        tops, sums, deltas = [], [], []
+        for b in range(blocks):
+            here = slice(b * 128, (b + 1) * 128)
+            at = pl.ds(pl.multiple_of(first + b * 128, 128), 128)
+            s = dot(ka[at, :], q_tile, NT)
+            if b == blocks - 1:
+                key_at = lax.broadcasted_iota(jnp.int32, (128, ROW_TILE), 0)
+                query_at = lax.broadcasted_iota(jnp.int32, (128, ROW_TILE), 1) % 128
+                s = jnp.where(key_at <= query_at, s, masked_bias)
+            top = jnp.max(s, axis=0, keepdims=True)
+            e = jnp.exp2((s - top) * exp2_scale)
+            d = dot(va[at, :], g_tile, NT)
+            s_scr[here, lanes] = e
+            d_scr[here, lanes] = d
+            tops.append(top)
+            sums.append(jnp.sum(e, axis=0, keepdims=True))
+            deltas.append(jnp.sum(e * d, axis=0, keepdims=True))
+        best = tops[0]
+        for b in range(1, blocks):
+            best = jnp.maximum(best, tops[b])
+        factors = [jnp.exp2((top - best) * exp2_scale) for top in tops]
+        inverse = 1.0 / sum(f * x for f, x in zip(factors, sums))
+        row_delta = sum(f * x for f, x in zip(factors, deltas)) * inverse
+        for b in range(blocks):
+            here = slice(b * 128, (b + 1) * 128)
+            p = s_scr[here, lanes] * (factors[b] * inverse)
+            p_scr[here, lanes] = p.astype(jnp.bfloat16)
+            ds_scr[here, lanes] = (p * (d_scr[here, lanes] - row_delta)).astype(jnp.bfloat16)
     window = pl.ds(first, blocks * 128)
-    dv_acc[window, :] += dot(p_scr[...], g_all, NN)
-    dk_acc[window, :] += dot(ds_scr[...], q_all[:, :128], NN)
+    dv_acc[window, :] += dot(p_scr[...], ga[...], NN)
+    dk_acc[window, :] += dot(ds_scr[...], qa[:, :128], NN)
     dq_t = dot(kt[:, window], ds_scr[...], NN) * score_scale
 
     @pl.when(slot == 0)
@@ -153,10 +157,10 @@
 
     @pl.when((slot == 1) & (step == steps - 1))
     def _():
-        for i in range(DOC_LIMIT // 256):
+        for i, block in enumerate((dkv_4, dkv_3, dkv_2, dkv_1)):
             at = slice(i * 256, (i + 1) * 256)
-            dkv_halo[i, :, :128] = (dk_acc[at, :] * score_scale).astype(jnp.bfloat16)
-            dkv_halo[i, :, 128:] = dv_acc[at, :].astype(jnp.bfloat16)
+            block[:, :128] = (dk_acc[at, :] * score_scale).astype(jnp.bfloat16)
+            block[:, 128:] = dv_acc[at, :].astype(jnp.bfloat16)
         dkv_own[:, :128] = dk_acc[DOC_LIMIT:, :] * score_scale
         dkv_own[:, 128:] = dv_acc[DOC_LIMIT:, :]
 
@@ -192,14 +196,20 @@
                 pl.BlockSpec((128, width), other),
                 pl.BlockSpec((128, width), other),
                 pl.BlockSpec((256, 256), fixed(2)),
-                pl.BlockSpec((DOC_LIMIT // 256, 256, 256), fixed(3)),
+                pl.BlockSpec((256, 256), fixed(2)),
+                pl.BlockSpec((256, 256), fixed(2)),
+                pl.BlockSpec((256, 256), fixed(2)),
+                pl.BlockSpec((256, 256), fixed(2)),
                 pl.BlockSpec((window, 128), fixed(2)),
                 pl.BlockSpec((1, 128, 128), lambda s, j, c: (s, 0, 0)),
             ],
             out_specs=[
                 pl.BlockSpec((128, width), own_out),
                 pl.BlockSpec((128, width), other),
-                pl.BlockSpec((DOC_LIMIT // 256, 256, 256), fixed(3)),
+                pl.BlockSpec((256, 256), fixed(2)),
+                pl.BlockSpec((256, 256), fixed(2)),
+                pl.BlockSpec((256, 256), fixed(2)),
+                pl.BlockSpec((256, 256), fixed(2)),
                 pl.BlockSpec((256, 256), fixed(2)),
             ],
             scratch_shapes=[
@@ -219,18 +229,21 @@
         out_shape=[
             jax.ShapeDtypeStruct((128, GROUP_COLS), bf16),
             jax.ShapeDtypeStruct((128, GROUP_COLS), bf16),
-            jax.ShapeDtypeStruct((DOC_LIMIT // 256, 256, 256), bf16),
+            jax.ShapeDtypeStruct((256, 256), bf16),
+            jax.ShapeDtypeStruct((256, 256), bf16),
+            jax.ShapeDtypeStruct((256, 256), bf16),
+            jax.ShapeDtypeStruct((256, 256), bf16),
             jax.ShapeDtypeStruct((256, 256), f32),
         ],
         compiler_params=pltpu.CompilerParams(
-            dimension_semantics=("arbitrary", "arbitrary"), vmem_limit_bytes=40 * 1024 * 1024
+            dimension_semantics=("arbitrary", "arbitrary"), vmem_limit_bytes=56 * 1024 * 1024
         ),
         cost_estimate=pl.CostEstimate(
             flops=12 * 2 * 16 * 128 * keys * 128,
             bytes_accessed=5 << 20,
             transcendentals=32 * 128 * keys,
         ),
-    )(core, queries, grads, q_other, g_other, kv_own, kv_halo, key_mark, query_mark)
+    )(core, queries, grads, q_other, g_other, kv_own, *kv_halo, key_mark, query_mark)
 
 
 def on_device(
@@ -268,12 +281,10 @@
         jnp.concatenate([kv_mine, kv_got], axis=0),
         jnp.concatenate([kv_got, kv_mine], axis=0),
     )
-    kv_halo = jnp.stack(
-        [
-            lax.ppermute(kv_own, "seq", [(i, i + 2 * d) for i in range(seq_size - 2 * d)])
-            for d in range(halo_chips, 0, -1)
-        ]
-    )
+    kv_halo = [
+        lax.ppermute(kv_own, "seq", [(i, i + 2 * d) for i in range(seq_size - 2 * d)])
+        for d in range(1, halo_chips + 1)
+    ]
     q_other = lax.ppermute(head_cols(queries, 1 - core, GROUP_COLS), "seq", swap_cores)
     g_other = lax.ppermute(head_cols(output_gradient, 1 - core, GROUP_COLS), "seq", swap_cores)
 
@@ -297,15 +308,6 @@
     )
     column_scale = jnp.repeat(row_scale, SCALE_BLOCK_SIDE, axis=1)
     weight_rows = decode_rows(weight_codes, column_scale)
-    crossed = lax.ppermute(
-        weight_rows,
-        ("dp", "seq"),
-        [
-            (a * seq_size + b, b * seq_size + a)
-            for a in range(dp_size)
-            for b in range(seq_size)
-        ],
-    )
     x_size = 4
     x_at, z_at = dp_idx % x_size, dp_idx // x_size
     z_size = dp_size // x_size
@@ -318,20 +320,10 @@
     def z_turn(d):
         return [(i, (i // x_size + d) % z_size * x_size + i % x_size) for i in range(dp_size)]
 
-    def ring_gather(block, turn, size, at):
-        parts = [block] + [lax.ppermute(block, "dp", turn(d)) for d in range(1, size)]
-        stacked = jnp.stack(parts[::-1] + parts[:0:-1])
-        return lax.dynamic_slice_in_dim(stacked, size - 1 - at, size, 0)
-
-    weight_row = ring_gather(crossed, x_turn, x_size, x_at)
-    weight_block = ring_gather(weight_row, z_turn, z_size, z_at).reshape(
-        dp_size * rows_dev, weight_rows.shape[1]
-    )
-    own_cols = jnp.concatenate(
-        [head_cols(weight_block, core, 128), head_cols(weight_block, 2 + core, 128)], axis=1
-    )
-    other_cols = jnp.concatenate(
-        [head_cols(weight_block, 1 - core, 128), head_cols(weight_block, 3 - core, 128)], axis=1
+    weight_block = (
+        lax.all_gather(jnp.tile(weight_rows, (WIDEN, 1)), "dp", axis=0, tiled=True)
+        .reshape(dp_size, WIDEN, rows_dev, weight_rows.shape[1])[:, 0]
+        .reshape(dp_size * rows_dev, weight_rows.shape[1])
     )
 
     tokens = activations.shape[0]
@@ -341,11 +333,10 @@
         .transpose(1, 0, 2, 3)
         .reshape(seq_size, dp_size * piece, tokens)
     )
-    act_rows, _ = lax.optimization_barrier((act_rows, kv_halo))
-    act_all = lax.all_to_all(act_rows, "seq", split_axis=0, concat_axis=0)
-    act_all = act_all.transpose(1, 0, 2).reshape(dp_size * piece, seq_size * tokens)
-
-    dq_own, dq_other, dkv_halo, dkv_own = attend_grads(
+    act_rows, *kv_halo = lax.optimization_barrier((act_rows, *kv_halo))
+    arrived = lax.all_to_all(act_rows, "seq", split_axis=0, concat_axis=0)
+
+    dq_own, dq_other, *dkv_halo, dkv_own = attend_grads(
         core.reshape(1), queries, output_gradient, q_other, g_other, kv_own, kv_halo,
         key_mark, query_mark,
     )
@@ -356,16 +347,15 @@
         jnp.concatenate([dq_back, dq_own], axis=1),
     )
 
-    dkv_halo, dkv_own, act_all, own_cols, other_cols = lax.optimization_barrier(
-        (dkv_halo, dkv_own, act_all, own_cols, other_cols)
-    )
+    arrived_now, dkv_own, *dkv_halo = lax.optimization_barrier((arrived, dkv_own, *dkv_halo))
+    act_all = arrived_now.transpose(1, 0, 2).reshape(dp_size * piece, seq_size * tokens)
     kv_sum = dkv_own
     for d in range(1, halo_chips + 1):
         part = lax.ppermute(
-            dkv_halo[halo_chips - d], "seq", [(i, i - 2 * d) for i in range(2 * d, seq_size)]
+            dkv_halo[d - 1], "seq", [(i, i - 2 * d) for i in range(2 * d, seq_size)]
         )
         kv_sum = kv_sum + part.astype(f32)
-    kv_chip = kv_sum.astype(bf16)
+    kv_chip, weight_block = lax.optimization_barrier((kv_sum.astype(bf16), weight_block))
     kv_group = lax.all_to_all(
         jnp.broadcast_to(kv_chip[None], (chips,) + kv_chip.shape),
         "seq",
@@ -374,7 +364,6 @@
         axis_index_groups=same_core,
     ).reshape(chips * 256, 256)
     kv_swap = lax.ppermute(kv_group, "seq", swap_cores)
-    grad_x_cols = (dot(kv_group, own_cols, NT) + dot(kv_swap, other_cols, NT)).astype(bf16)
     weight_part = jnp.concatenate(
         [dot(act_all, kv_group, NN), dot(act_all, kv_swap, NN)], axis=1
     ).astype(bf16)
@@ -395,7 +384,22 @@
         jnp.concatenate([own_k, other_k, own_v, other_v], axis=1),
         jnp.concatenate([other_k, own_k, other_v, own_v], axis=1),
     )
-    grad_x = lax.all_to_all(grad_x_cols, "seq", split_axis=0, concat_axis=1, tiled=True)
+    def cols_of(which):
+        return jnp.concatenate(
+            [head_cols(weight_block, which, 128), head_cols(weight_block, 2 + which, 128)], axis=1
+        )
+
+    grad_x_rows = (
+        dot(cols_of(core), kv_group, NT) + dot(cols_of(1 - core), kv_swap, NT)
+    ).astype(bf16)
+    grad_x_rows = grad_x_rows.reshape(dp_size * piece, seq_size, tokens).transpose(1, 0, 2)
+    grad_x = lax.all_to_all(grad_x_rows, "seq", split_axis=0, concat_axis=0)
+    grad_x = (
+        grad_x.reshape(seq_size, dp_size, piece, tokens)
+        .transpose(1, 0, 2, 3)
+        .reshape(dp_size * seq_size * piece, tokens)
+        .T
+    )
     return (grad_q, grad_x, grad_weights)
 
 

time: 177 us -> 145 us (0.82)
  starting transfers between devices: 64.8 us -> 44.8 us
  between operations: 1.11 us -> 14.4 us
  local copies, waits for them, and re-layouts: 24.5 us -> 14.2 us
  Pallas kernels: 31.1 us -> 21 us
  waiting for transfers between devices: 22.4 us -> 18.8 us
  matrix products: 7.44 us -> 5.19 us
    ppermute x11 -> x4, starting transfers between devices: 25.6 us -> 7.87 us  [on_device(): lax.ppermute(dkv_halo[d - 1], 'seq', [(i, i - 2 * d) for i in range(2 * d...]
    all_gather x0 -> x1, waiting for transfers between devices: none -> 12.6 us  [on_device(): lax.all_gather(jnp.tile(weight_rows, (WIDEN, 1)), 'dp', axis=0, tiled=True)]
    ppermute x11 -> x4, waiting for transfers between devices: 12.5 us -> 0.01 us  [on_device(): lax.ppermute(dkv_halo[d - 1], 'seq', [(i, i - 2 * d) for i in range(2 * d...]
    pallas_call x1, Pallas kernels: 31.1 us -> 21 us  [attend_grads(): pl.pallas_call(attention_kernel, grid_spec=pltpu.PrefetchScalarGridSpec(n...]
    unnamed x33 -> x20, local copies, waits for them, and re-layouts: 10.5 us -> 4.44 us
    all_to_all x2, starting transfers between devices: 15 us -> 10.2 us  [the longest x1 5.34 us: on_device(): grad_x = lax.all_to_all(grad_x_rows, 'seq', split_axis=0, concat_axis=0)]
    ppermute x6, starting transfers between devices: 9.63 us -> 13.5 us  [ring_scatter(): total = total + lax.ppermute(block.astype(bf16), 'dp', turn(d)).astype(f32)]
    ppermute x6, waiting for transfers between devices: 7.28 us -> 4.49 us  [ring_scatter(): total = total + lax.ppermute(block.astype(bf16), 'dp', turn(d)).astype(f32)]
  transfers between devices with their start and end apart: 28 -> 22, of which waited for: 8 -> 7; matrix products, arithmetic and copies ran while one was open for 15% -> 15% of each run, Pallas kernels for 18% -> 15%
where the time goes in v3:
time: 145 us; the launch traced here: 144 us
  starting transfers between devices  44.8 us (31%)
  Pallas kernels  21 us (14%)
  waiting for transfers between devices  18.8 us (13%)
  blocking collectives  18.6 us (13%)
  between operations  14.4 us (10%)
  local copies, waits for them, and re-layouts  14.2 us (10%)
  other arithmetic  6.72 us (5%)
  matrix products  5.19 us (4%)
    pallas_call x1, Pallas kernels, attend_grads(): pl.pallas_call(attention_kernel, grid_spec=pltpu.PrefetchScalarGridSpec(n...  21 us
    all_to_all x1, blocking collectives, on_device(): lax.all_to_all(jnp.broadcast_to(kv_chip[None], (chips,) + kv_chip.shape),...  18.6 us
    ppermute x6, starting transfers between devices, ring_scatter(): total = total + lax.ppermute(block.astype(bf16), 'dp', turn(d)).astype(f32)  13.5 us
    all_gather x1, waiting for transfers between devices, on_device(): lax.all_gather(jnp.tile(weight_rows, (WIDEN, 1)), 'dp', axis=0, tiled=True)  12.6 us
    ppermute x4, starting transfers between devices, on_device(): lax.ppermute(kv_own, 'seq', [(i, i + 2 * d) for i in range(seq_size - 2 *...  11.9 us
    ppermute x4, starting transfers between devices, on_device(): lax.ppermute(dkv_halo[d - 1], 'seq', [(i, i - 2 * d) for i in range(2 * d...  7.87 us
    all_to_all x1, starting transfers between devices, on_device(): grad_x = lax.all_to_all(grad_x_rows, 'seq', split_axis=0, concat_axis=0)  5.34 us
    all_to_all x1, starting transfers between devices, on_device(): arrived = lax.all_to_all(act_rows, 'seq', split_axis=0, concat_axis=0)  4.81 us
  transfers between devices with their start and end apart: 22, of which 7 were waited for; matrix products, arithmetic and copies ran while one was open for 15% of the time, Pallas kernels for 15%

profile of v3, /device:TPU:8, one launch (start us, length us, event | category | flops | bytes accessed | tf_op | source)
XLA Modules:
  0.0 143.7 jit_solution(17737502568015992387)
XLA Ops:
  7.2 0.0 all-gather.2.cloned.1.call-start
  7.2 0.8 constant_dynamic-slice_fusion.8
  8.1 0.1 collective-permute-start.2
  8.2 0.9 fusion.44
  9.1 0.3 collective-permute-done.2
  9.5 4.2 %collective-permute-start.6 = (bf16[256,256]{1,0:T(8,128)(2,1)S(1)}, bf16[256,256]{1,0:T(8,128)(2,1)S(1)}, u32[]{:S(2)}, u32[]{:S(2)}) collective-permute-start(bf16[256,256]{1,0:T(8,128)(2,1)S(1)} %maximum_select_fusion.1.kv_own), channel_id=1, source_target_pairs={{0,8},{1,9},{2,10},{3,11},{4,12},{5,13},{6,14},{7,15},{16,24},{17,... | collective-permute-start | bytes 393224 | tf_op jit(solution)/shard_map/ppermute | solution.py:285
  13.7 1.9 %collective-permute-start.5 = (bf16[256,256]{1,0:T(8,128)(2,1)S(1)}, bf16[256,256]{1,0:T(8,128)(2,1)S(1)}, u32[]{:S(2)}, u32[]{:S(2)}) collective-permute-start(bf16[256,256]{1,0:T(8,128)(2,1)S(1)} %maximum_select_fusion.1.kv_own), channel_id=1, source_target_pairs={{0,6},{1,7},{2,8},{3,9},{4,10},{5,11},{6,12},{7,13},{8,14},{9,15},... | collective-permute-start | bytes 393224 | tf_op jit(solution)/shard_map/ppermute | solution.py:285
  15.6 3.2 %collective-permute-start.4 = (bf16[256,256]{1,0:T(8,128)(2,1)S(1)}, bf16[256,256]{1,0:T(8,128)(2,1)S(1)}, u32[]{:S(2)}, u32[]{:S(2)}) collective-permute-start(bf16[256,256]{1,0:T(8,128)(2,1)S(1)} %maximum_select_fusion.1.kv_own), channel_id=1, source_target_pairs={{0,4},{1,5},{2,6},{3,7},{4,8},{5,9},{6,10},{7,11},{8,12},{9,13},{1... | collective-permute-start | bytes 393224 | tf_op jit(solution)/shard_map/ppermute | solution.py:285
  18.8 2.6 %collective-permute-start.3 = (bf16[256,256]{1,0:T(8,128)(2,1)S(1)}, bf16[256,256]{1,0:T(8,128)(2,1)S(1)}, u32[]{:S(2)}, u32[]{:S(2)}) collective-permute-start(bf16[256,256]{1,0:T(8,128)(2,1)S(1)} %maximum_select_fusion.1.kv_own), channel_id=1, source_target_pairs={{0,2},{1,3},{2,4},{3,5},{4,6},{5,7},{6,8},{7,9},{8,10},{9,11},{10,... | collective-permute-start | bytes 393224 | tf_op jit(solution)/shard_map/ppermute | solution.py:285
  21.4 0.1 broadcast_in_dim.14
  21.5 0.8 fusion.27
  22.3 0.6 tile.4
  22.9 0.0 all-gather.2.cloned.1.call-update
  22.9 1.6 %copy.17 = bf16[128,4096]{0,1:T(8,128)(2,1)S(1)} copy(bf16[128,4096]{1,0:T(8,128)(2,1)} %param.8) | data formatting | bytes 2097152 | tf_op args[0]
  24.6 1.2 copy.18
  25.8 0.0 collective-permute-done.6.kv_4
  25.8 0.0 collective-permute-done.5.kv_3
  25.9 1.1 collective-permute-done.4.kv_2
  27.0 0.6 copy-done.7
  27.6 0.1 copy-done.8
  27.7 4.8 %all-to-all-start = ((bf16[16,256,128]{2,1,0:T(8,128)(2,1)}), bf16[16,256,128]{2,1,0:T(8,128)(2,1)S(1)}, u32[]{:S(2)}, u32[]{:S(2)}) async-start(bf16[16,256,128]{2,1,0:T(8,128)(2,1)} %bitcast.4), calls=%async_computation | async-start | bytes 2097152 | tf_op jit(solution)/shard_map/all_to_all | solution.py:337
  32.5 1.1 constant_dynamic-slice_fusion.10
  33.6 0.2 collective-permute-start.1
  33.9 0.4 collective-permute-start
  34.4 0.7 select_convert_fusion.query_mark
  35.1 0.1 pad_dynamic-slice_fusion.8
  35.2 1.0 fusion.3.key_mark
  36.1 0.2 collective-permute-done.q_other
  36.3 0.8 copy-done.4
  37.1 21.0 %shard_map.103 = (bf16[128,2048]{1,0:T(8,128)(2,1)}, bf16[128,2048]{1,0:T(8,128)(2,1)}, bf16[256,256]{1,0:T(8,128)(2,1)}, bf16[256,256]{1,0:T(8,128)(2,1)}, bf16...) custom-call(s32[1]{0:T(128)} %bitcast.core_ref, bf16[128,4096]{1,0:T(8,128)(2,1)} %q_own.1, ...), custom_call_target="tpu_custom_call" | custom-call | flops 7247757312 | bytes 5242880 | tf_op jit(solution)/shard_map/pallas_call | solution.py:188
  58.1 0.0 all-to-all-done
  58.2 3.4 %collective-permute-start.8 = (bf16[256,256]{1,0:T(8,128)(2,1)}, bf16[256,256]{1,0:T(8,128)(2,1)S(1)}, u32[]{:S(2)}, u32[]{:S(2)}) collective-permute-start(bf16[256,256]{1,0:T(8,128)(2,1)} %get-tuple-element.36), channel_id=1, source_target_pairs={{2,0},{3,1},{4,2},{5,3},{6,4},{7,5},{8,6},{9,7},{10,8},{11,9},{12,... | collective-permute-start | bytes 393224 | tf_op jit(solution)/shard_map/ppermute | solution.py:354
  61.5 1.9 %collective-permute-start.9 = (bf16[256,256]{1,0:T(8,128)(2,1)}, bf16[256,256]{1,0:T(8,128)(2,1)S(1)}, u32[]{:S(2)}, u32[]{:S(2)}) collective-permute-start(bf16[256,256]{1,0:T(8,128)(2,1)} %get-tuple-element.37), channel_id=1, source_target_pairs={{4,0},{5,1},{6,2},{7,3},{8,4},{9,5},{10,6},{11,7},{12,8},{13,9},{1... | collective-permute-start | bytes 393224 | tf_op jit(solution)/shard_map/ppermute | solution.py:354
  63.5 1.3 collective-permute-start.10
  64.8 1.3 collective-permute-start.11
  66.1 12.6 %all-gather.2.cloned.1.call-done = bf16[1024,512]{1,0:T(8,128)(2,1)} async-done(((bf16[64,512]{1,0:T(8,128)(2,1)}), bf16[1024,512]{1,0:T(8,128)(2,1)}) %all-gather.2.cloned.1.call-update) | async-done | bytes 1048592 | tf_op jit(solution)/shard_map/all_gather | solution.py:324
  78.6 1.0 slice.20
  79.6 0.0 collective-permute-done.8
  79.6 1.0 add_convert_fusion
  80.7 0.1 broadcast_in_dim.15
  80.7 18.6 %all_to_all.15 = bf16[8,256,256]{2,1,0:T(8,128)(2,1)S(1)} all-to-all(bf16[8,256,256]{2,1,0:T(8,128)(2,1)S(1)} %broadcast_in_dim.15), channel_id=1, replica_groups={{0,2,4,6,8,10,12,14},{1,3,5,7,9,11,13,15},{16,18,20,22,24,26,28,30},{17..., dimensions={0} | all-to-all | bytes 2097152 | tf_op jit(solution)/shard_map/all_to_all | solution.py:359
  99.4 0.5 collective-permute-start.7
  99.9 1.6 %copy.22 = bf16[256,16,128]{2,1,0:T(8,128)(2,1)} copy(bf16[256,16,128]{2,0,1:T(8,128)(2,1)S(1)} %bitcast.70) | data formatting | bytes 2097152 | tf_op jit(solution)/shard_map/transpose | solution.py:351
  101.5 1.5 %dot_general.20 = bf16[4,4,16,2048]{3,2,1,0:T(8,128)(2,1)S(1)} reshape(bf16[256,16,128]{2,1,0:T(8,128)(2,1)} %copy.22) | data formatting | bytes 2097152 | tf_op jit(solution)/shard_map/dot_general | solution.py:30
  103.1 0.1 constant_dynamic-slice_fusion.1
  103.1 0.5 fusion.4
  103.6 1.7 %fusion.1 = bf16[32,16,8,128]{3,2,1,0:T(8,128)(2,1)S(1)} fusion(f32[256,2048]{1,0:T(8,128)S(1)} %fusion.4, bf16[2048,256]{1,0:T(8,128)(2,1)} %collective-permute-done.12, bf16[256,128]{1,0:T(8,128)(2,1)S(1)} %get-tuple-element.53, bf16[256,128]{1,0:T(8,128)(2,1)S(1)} %get-tuple-element.52), kind=kOutput, calls=%fused_computation.2 | convolution fusion | flops 269746176 | bytes 4325376 | tf_op jit(solution)/shard_map/dot_general | solution.py:30
  105.3 1.2 copy.31
  106.6 5.3 %all-to-all-start.2 = ((bf16[16,256,128]{2,1,0:T(8,128)(2,1)}), bf16[16,256,128]{2,1,0:T(8,128)(2,1)S(1)}, u32[]{:S(2)}, u32[]{:S(2)}) async-start(bf16[16,256,128]{2,1,0:T(8,128)(2,1)} %bitcast.72), calls=%async_computation.2 | async-start | bytes 2097152 | tf_op jit(solution)/shard_map/all_to_all | solution.py:396
  111.9 0.4 convolution_convert_fusion.1
  112.4 1.7 %convolution_convert_fusion = bf16[4,4,16,256]{3,2,1,0:T(8,128)(2,1)S(1)} fusion(bf16[4,4,16,2048]{3,2,1,0:T(8,128)(2,1)S(1)} %dot_general.20, bf16[2048,256]{1,0:T(8,128)(2,1)} %collective-permute-done.12), kind=kOutput, calls=%fused_computation.3 | convolution fusion | flops 268500992 | bytes 2228224 | tf_op jit(solution)/shard_map/dot_general | solution.py:30
  114.1 1.4 %collective-permute-start.13 = (bf16[4,16,512]{2,1,0:T(8,128)(2,1)S(1)}, bf16[4,16,512]{2,1,0:T(8,128)(2,1)S(1)}, u32[]{:S(2)}, u32[]{:S(2)}) collective-permute-start(bf16[4,16,512]{2,1,0:T(8,128)(2,1)S(1)} %get-tuple-element.49), channel_id=1, source_target_pairs={{0,16},{16,32},{32,48},{48,0},{64,80},{80,96},{96,112},{112,64},{1... | collective-permute-start | bytes 196616 | tf_op jit(solution)/shard_map/ppermute | solution.py:375
  115.5 2.9 %collective-permute-start.14 = (bf16[4,16,512]{2,1,0:T(8,128)(2,1)S(1)}, bf16[4,16,512]{2,1,0:T(8,128)(2,1)S(1)}, u32[]{:S(2)}, u32[]{:S(2)}) collective-permute-start(bf16[4,16,512]{2,1,0:T(8,128)(2,1)S(1)} %get-tuple-element.50), channel_id=1, source_target_pairs={{0,32},{16,48},{32,0},{48,16},{64,96},{80,112},{96,64},{112,80},{1... | collective-permute-start | bytes 196616 | tf_op jit(solution)/shard_map/ppermute | solution.py:375
  118.4 1.4 collective-permute-start.15
  119.9 2.1 %collective-permute-done.14 = bf16[4,16,512]{2,1,0:T(8,128)(2,1)S(1)} collective-permute-done((bf16[4,16,512]{2,1,0:T(8,128)(2,1)S(1)}, bf16[4,16,512]{2,1,0:T(8,128)(2,1)S(1)}, u32[]{:S(2)}, u32[]{:S(2)}) %collective-permute-start.14) | collective-permute-done | bytes 65568 | tf_op jit(solution)/shard_map/ppermute | solution.py:375
  122.0 0.7 collective-permute-done.15
  122.8 1.3 collective-permute-start.16
  124.1 2.9 %collective-permute-start.18 = (bf16[16,512]{1,0:T(8,128)(2,1)S(1)}, bf16[16,512]{1,0:T(8,128)(2,1)S(1)}, u32[]{:S(2)}, u32[]{:S(2)}) collective-permute-start(bf16[16,512]{1,0:T(8,128)(2,1)S(1)} %get-tuple-element.57), channel_id=1, source_target_pairs={{0,192},{16,208},{32,224},{48,240},{64,0},{80,16},{96,32},{112,48}... | collective-permute-start | bytes 49160 | tf_op jit(solution)/shard_map/ppermute | solution.py:375
  127.0 3.6 %collective-permute-start.17 = (bf16[16,512]{1,0:T(8,128)(2,1)S(1)}, bf16[16,512]{1,0:T(8,128)(2,1)S(1)}, u32[]{:S(2)}, u32[]{:S(2)}) collective-permute-start(bf16[16,512]{1,0:T(8,128)(2,1)S(1)} %get-tuple-element.58), channel_id=1, source_target_pairs={{0,128},{16,144},{32,160},{48,176},{64,192},{80,208},{96,224},{112... | collective-permute-start | bytes 49160 | tf_op jit(solution)/shard_map/ppermute | solution.py:375
  130.6 2.4 %maximum_select_fusion = bf16[128,4096]{1,0:T(8,128)(2,1)} fusion(bf16[128,2048]{1,0:T(8,128)(2,1)} %collective-permute-done.7, bf16[128,2048]{1,0:T(8,128)(2,1)S(1)} %copy-done, pred[]{:T(512)S(6)} %eq.56), kind=kLoop, calls=%fused_computation.6 | loop fusion | flops 4718592 | bytes 2097153 | tf_op jit(solution)/shard_map/jit(_where)/select_n | solution.py:344
  133.0 1.6 %collective-permute-done.17 = bf16[16,512]{1,0:T(8,128)(2,1)S(1)} collective-permute-done((bf16[16,512]{1,0:T(8,128)(2,1)S(1)}, bf16[16,512]{1,0:T(8,128)(2,1)S(1)}, u32[]{:S(2)}, u32[]{:S(2)}) %collective-permute-start.17) | collective-permute-done | bytes 16416 | tf_op jit(solution)/shard_map/ppermute | solution.py:375
  134.7 0.6 maximum_select_fusion.2
  135.3 0.3 copy.21
  135.6 1.3 copy.23
  (38 shorter events, 0.3 us)
Async XLA Ops:
  7.2 71.5 %all-gather.2.cloned.1.call-start = ((), (), s32[]{:S(2)}) async-start(), calls=%async_computation.3 | async-start | bytes 1114112 | tf_op jit(solution)/shard_map/all_gather | solution.py:324
  8.1 1.3 collective-permute-start.2
  9.5 16.4 %copy-start.2 = (bf16[256,256]{1,0:T(8,128)(2,1)}, bf16[256,256]{1,0:T(8,128)(2,1)S(1)}, u32[]{:S(2)}) copy-start(bf16[256,256]{1,0:T(8,128)(2,1)S(1)} %maximum_select_fusion.1.kv_own) | copy-start | bytes 393220
  9.5 16.4 %collective-permute-start.6 = (bf16[256,256]{1,0:T(8,128)(2,1)S(1)}, bf16[256,256]{1,0:T(8,128)(2,1)S(1)}, u32[]{:S(2)}, u32[]{:S(2)}) collective-permute-start(bf16[256,256]{1,0:T(8,128)(2,1)S(1)} %maximum_select_fusion.1.kv_own), channel_id=1, source_target_pairs={{0,8},{1,9},{2,10},{3,11},{4,12},{5,13},{6,14},{7,15},{16,24},{17,... | collective-permute-start | bytes 393224 | tf_op jit(solution)/shard_map/ppermute | solution.py:285
  13.7 12.2 %collective-permute-start.5 = (bf16[256,256]{1,0:T(8,128)(2,1)S(1)}, bf16[256,256]{1,0:T(8,128)(2,1)S(1)}, u32[]{:S(2)}, u32[]{:S(2)}) collective-permute-start(bf16[256,256]{1,0:T(8,128)(2,1)S(1)} %maximum_select_fusion.1.kv_own), channel_id=1, source_target_pairs={{0,6},{1,7},{2,8},{3,9},{4,10},{5,11},{6,12},{7,13},{8,14},{9,15},... | collective-permute-start | bytes 393224 | tf_op jit(solution)/shard_map/ppermute | solution.py:285
  15.6 11.4 %collective-permute-start.4 = (bf16[256,256]{1,0:T(8,128)(2,1)S(1)}, bf16[256,256]{1,0:T(8,128)(2,1)S(1)}, u32[]{:S(2)}, u32[]{:S(2)}) collective-permute-start(bf16[256,256]{1,0:T(8,128)(2,1)S(1)} %maximum_select_fusion.1.kv_own), channel_id=1, source_target_pairs={{0,4},{1,5},{2,6},{3,7},{4,8},{5,9},{6,10},{7,11},{8,12},{9,13},{1... | collective-permute-start | bytes 393224 | tf_op jit(solution)/shard_map/ppermute | solution.py:285
  18.8 8.2 %collective-permute-start.3 = (bf16[256,256]{1,0:T(8,128)(2,1)S(1)}, bf16[256,256]{1,0:T(8,128)(2,1)S(1)}, u32[]{:S(2)}, u32[]{:S(2)}) collective-permute-start(bf16[256,256]{1,0:T(8,128)(2,1)S(1)} %maximum_select_fusion.1.kv_own), channel_id=1, source_target_pairs={{0,2},{1,3},{2,4},{3,5},{4,6},{5,7},{6,8},{7,9},{8,10},{9,11},{10,... | collective-permute-start | bytes 393224 | tf_op jit(solution)/shard_map/ppermute | solution.py:285
  25.8 8.0 %copy-start.1 = (bf16[128,4096]{1,0:T(8,128)(2,1)S(1)}, bf16[128,4096]{1,0:T(8,128)(2,1)}, u32[]{:S(2)}) copy-start(bf16[128,4096]{1,0:T(8,128)(2,1)} %q_own.1) | copy-start | bytes 3145732
  25.8 8.0 %copy-start.5 = (bf16[256,256]{1,0:T(8,128)(2,1)}, bf16[256,256]{1,0:T(8,128)(2,1)S(1)}, u32[]{:S(2)}) copy-start(bf16[256,256]{1,0:T(8,128)(2,1)S(1)} %collective-permute-done.6.kv_4) | copy-start | bytes 393220
  25.8 8.0 %copy-start.6 = (bf16[256,256]{1,0:T(8,128)(2,1)}, bf16[256,256]{1,0:T(8,128)(2,1)S(1)}, u32[]{:S(2)}) copy-start(bf16[256,256]{1,0:T(8,128)(2,1)S(1)} %collective-permute-done.5.kv_3) | copy-start | bytes 393220
  27.0 0.7 copy-start.7
  27.0 0.7 copy-start.8
  27.0 7.4 %copy-start.3 = (s32[1,2048]{1,0:T(1,128)S(1)}, s32[1,2048]{1,0:T(1,128)}, u32[]{:S(2)}) copy-start(s32[1,2048]{1,0:T(1,128)} %param.13) | copy-start | bytes 24580
  27.7 30.5 %all-to-all-start = ((bf16[16,256,128]{2,1,0:T(8,128)(2,1)}), bf16[16,256,128]{2,1,0:T(8,128)(2,1)S(1)}, u32[]{:S(2)}, u32[]{:S(2)}) async-start(bf16[16,256,128]{2,1,0:T(8,128)(2,1)} %bitcast.4), calls=%async_computation | async-start | bytes 2097152 | tf_op jit(solution)/shard_map/all_to_all | solution.py:337
  33.6 2.5 %collective-permute-start.1 = (bf16[128,2048]{1,0:T(8,128)(2,1)S(1)}, bf16[128,2048]{1,0:T(8,128)(2,1)}, u32[]{:S(2)}, u32[]{:S(2)}) collective-permute-start(bf16[128,2048]{1,0:T(8,128)(2,1)S(1)} %constant_dynamic-slice_fusion.10), channel_id=1, source_target_pairs={{0,1},{1,0},{2,3},{3,2},{4,5},{5,4},{6,7},{7,6},{8,9},{9,8},{10,11... | collective-permute-start | bytes 1572872 | tf_op jit(solution)/shard_map/ppermute | solution.py:289
  33.9 2.4 %collective-permute-start = (bf16[128,2048]{1,0:T(8,128)(2,1)S(1)}, bf16[128,2048]{1,0:T(8,128)(2,1)S(1)}, u32[]{:S(2)}, u32[]{:S(2)}) collective-permute-start(bf16[128,2048]{1,0:T(8,128)(2,1)S(1)} %constant_dynamic-slice_fusion.11), channel_id=1, source_target_pairs={{0,1},{1,0},{2,3},{3,2},{4,5},{5,4},{6,7},{7,6},{8,9},{9,8},{10,11... | collective-permute-start | bytes 1572872 | tf_op jit(solution)/shard_map/ppermute | solution.py:288
  36.3 0.8 copy-start.4
  58.2 21.4 %collective-permute-start.8 = (bf16[256,256]{1,0:T(8,128)(2,1)}, bf16[256,256]{1,0:T(8,128)(2,1)S(1)}, u32[]{:S(2)}, u32[]{:S(2)}) collective-permute-start(bf16[256,256]{1,0:T(8,128)(2,1)} %get-tuple-element.36), channel_id=1, source_target_pairs={{2,0},{3,1},{4,2},{5,3},{6,4},{7,5},{8,6},{9,7},{10,8},{11,9},{12,... | collective-permute-start | bytes 393224 | tf_op jit(solution)/shard_map/ppermute | solution.py:354
  61.5 18.1 %collective-permute-start.9 = (bf16[256,256]{1,0:T(8,128)(2,1)}, bf16[256,256]{1,0:T(8,128)(2,1)S(1)}, u32[]{:S(2)}, u32[]{:S(2)}) collective-permute-start(bf16[256,256]{1,0:T(8,128)(2,1)} %get-tuple-element.37), channel_id=1, source_target_pairs={{4,0},{5,1},{6,2},{7,3},{8,4},{9,5},{10,6},{11,7},{12,8},{13,9},{1... | collective-permute-start | bytes 393224 | tf_op jit(solution)/shard_map/ppermute | solution.py:354
  63.5 16.2 %collective-permute-start.10 = (bf16[256,256]{1,0:T(8,128)(2,1)}, bf16[256,256]{1,0:T(8,128)(2,1)S(1)}, u32[]{:S(2)}, u32[]{:S(2)}) collective-permute-start(bf16[256,256]{1,0:T(8,128)(2,1)} %get-tuple-element.38), channel_id=1, source_target_pairs={{6,0},{7,1},{8,2},{9,3},{10,4},{11,5},{12,6},{13,7},{14,8},{15,9},... | collective-permute-start | bytes 393224 | tf_op jit(solution)/shard_map/ppermute | solution.py:354
  64.8 14.9 %collective-permute-start.11 = (bf16[256,256]{1,0:T(8,128)(2,1)}, bf16[256,256]{1,0:T(8,128)(2,1)S(1)}, u32[]{:S(2)}, u32[]{:S(2)}) collective-permute-start(bf16[256,256]{1,0:T(8,128)(2,1)} %get-tuple-element.39), channel_id=1, source_target_pairs={{8,0},{9,1},{10,2},{11,3},{12,4},{13,5},{14,6},{15,7},{24,16},{25,... | collective-permute-start | bytes 393224 | tf_op jit(solution)/shard_map/ppermute | solution.py:354
  99.4 4.2 %collective-permute-start.12 = (bf16[2048,256]{1,0:T(8,128)(2,1)S(1)}, bf16[2048,256]{1,0:T(8,128)(2,1)}, u32[]{:S(2)}, u32[]{:S(2)}) collective-permute-start(bf16[2048,256]{1,0:T(8,128)(2,1)S(1)} %bitcast.67), channel_id=1, source_target_pairs={{0,1},{1,0},{2,3},{3,2},{4,5},{5,4},{6,7},{7,6},{8,9},{9,8},{10,11... | collective-permute-start | bytes 3145736 | tf_op jit(solution)/shard_map/ppermute | solution.py:366
  99.4 31.2 %collective-permute-start.7 = (bf16[128,2048]{1,0:T(8,128)(2,1)}, bf16[128,2048]{1,0:T(8,128)(2,1)}, u32[]{:S(2)}, u32[]{:S(2)}) collective-permute-start(bf16[128,2048]{1,0:T(8,128)(2,1)} %get-tuple-element.28), channel_id=1, source_target_pairs={{0,1},{1,0},{2,3},{3,2},{4,5},{5,4},{6,7},{7,6},{8,9},{9,8},{10,11... | collective-permute-start | bytes 1572872 | tf_op jit(solution)/shard_map/ppermute | solution.py:343
  106.6 28.7 %all-to-all-start.2 = ((bf16[16,256,128]{2,1,0:T(8,128)(2,1)}), bf16[16,256,128]{2,1,0:T(8,128)(2,1)S(1)}, u32[]{:S(2)}, u32[]{:S(2)}) async-start(bf16[16,256,128]{2,1,0:T(8,128)(2,1)} %bitcast.72), calls=%async_computation.2 | async-start | bytes 2097152 | tf_op jit(solution)/shard_map/all_to_all | solution.py:396
  112.3 18.2 %copy-start = (bf16[128,2048]{1,0:T(8,128)(2,1)S(1)}, bf16[128,2048]{1,0:T(8,128)(2,1)}, u32[]{:S(2)}) copy-start(bf16[128,2048]{1,0:T(8,128)(2,1)} %get-tuple-element.27) | copy-start | bytes 1572868
  114.1 5.8 %collective-permute-start.13 = (bf16[4,16,512]{2,1,0:T(8,128)(2,1)S(1)}, bf16[4,16,512]{2,1,0:T(8,128)(2,1)S(1)}, u32[]{:S(2)}, u32[]{:S(2)}) collective-permute-start(bf16[4,16,512]{2,1,0:T(8,128)(2,1)S(1)} %get-tuple-element.49), channel_id=1, source_target_pairs={{0,16},{16,32},{32,48},{48,0},{64,80},{80,96},{96,112},{112,64},{1... | collective-permute-start | bytes 196616 | tf_op jit(solution)/shard_map/ppermute | solution.py:375
  115.5 6.4 %collective-permute-start.14 = (bf16[4,16,512]{2,1,0:T(8,128)(2,1)S(1)}, bf16[4,16,512]{2,1,0:T(8,128)(2,1)S(1)}, u32[]{:S(2)}, u32[]{:S(2)}) collective-permute-start(bf16[4,16,512]{2,1,0:T(8,128)(2,1)S(1)} %get-tuple-element.50), channel_id=1, source_target_pairs={{0,32},{16,48},{32,0},{48,16},{64,96},{80,112},{96,64},{112,80},{1... | collective-permute-start | bytes 196616 | tf_op jit(solution)/shard_map/ppermute | solution.py:375
  118.4 4.3 %collective-permute-start.15 = (bf16[4,16,512]{2,1,0:T(8,128)(2,1)S(1)}, bf16[4,16,512]{2,1,0:T(8,128)(2,1)S(1)}, u32[]{:S(2)}, u32[]{:S(2)}) collective-permute-start(bf16[4,16,512]{2,1,0:T(8,128)(2,1)S(1)} %get-tuple-element.51), channel_id=1, source_target_pairs={{0,48},{16,0},{32,16},{48,32},{64,112},{80,64},{96,80},{112,96},{1... | collective-permute-start | bytes 196616 | tf_op jit(solution)/shard_map/ppermute | solution.py:375
  122.8 10.2 %collective-permute-start.16 = (bf16[16,512]{1,0:T(8,128)(2,1)S(1)}, bf16[16,512]{1,0:T(8,128)(2,1)S(1)}, u32[]{:S(2)}, u32[]{:S(2)}) collective-permute-start(bf16[16,512]{1,0:T(8,128)(2,1)S(1)} %get-tuple-element.56), channel_id=1, source_target_pairs={{0,64},{16,80},{32,96},{48,112},{64,128},{80,144},{96,160},{112,17... | collective-permute-start | bytes 49160 | tf_op jit(solution)/shard_map/ppermute | solution.py:375
  124.1 8.9 %collective-permute-start.18 = (bf16[16,512]{1,0:T(8,128)(2,1)S(1)}, bf16[16,512]{1,0:T(8,128)(2,1)S(1)}, u32[]{:S(2)}, u32[]{:S(2)}) collective-permute-start(bf16[16,512]{1,0:T(8,128)(2,1)S(1)} %get-tuple-element.57), channel_id=1, source_target_pairs={{0,192},{16,208},{32,224},{48,240},{64,0},{80,16},{96,32},{112,48}... | collective-permute-start | bytes 49160 | tf_op jit(solution)/shard_map/ppermute | solution.py:375
  127.0 7.6 %collective-permute-start.17 = (bf16[16,512]{1,0:T(8,128)(2,1)S(1)}, bf16[16,512]{1,0:T(8,128)(2,1)S(1)}, u32[]{:S(2)}, u32[]{:S(2)}) collective-permute-start(bf16[16,512]{1,0:T(8,128)(2,1)S(1)} %get-tuple-element.58), channel_id=1, source_target_pairs={{0,128},{16,144},{32,160},{48,176},{64,192},{80,208},{96,224},{112... | collective-permute-start | bytes 49160 | tf_op jit(solution)/shard_map/ppermute | solution.py:375
Sparse Core Ops, SparseCore 0:
  23.1 55.5 all-gather.1

commit v4 on v3

--- a/solution.py
+++ b/solution.py
@@ -14,7 +14,7 @@
 GROUP_HEADS = QUERY_HEADS // KEY_VALUE_HEADS
 GROUP_COLS = GROUP_HEADS * HEAD_WIDTH
 DOC_LIMIT = 1024
-HEADS_STEP = 8
+HEADS_STEP = 16
 WIDEN = 4
 ROW_TILE = 256
 
@@ -275,6 +275,35 @@
     kv_theirs = jnp.concatenate(
         [head_cols(saved_keys, 1 - core, 128), head_cols(saved_values, 1 - core, 128)], axis=1
     )
+    rows_dev = weight_codes.shape[0]
+    first_global = (dp_idx * seq_size + seq_idx) * rows_dev
+    row_block = (first_global + jnp.arange(rows_dev)) // SCALE_BLOCK_SIDE
+    row_pick = (row_block[:, None] == jnp.arange(exponents.shape[0])[None, :]).astype(f32)
+    row_scale = jnp.dot(
+        row_pick, jnp.exp2(exponents.astype(f32)), precision=lax.Precision.HIGHEST
+    )
+    column_scale = jnp.repeat(row_scale, SCALE_BLOCK_SIDE, axis=1)
+    weight_rows = decode_rows(weight_codes, column_scale)
+    x_size = 4
+    x_at, z_at = dp_idx % x_size, dp_idx // x_size
+    z_size = dp_size // x_size
+
+    def x_turn(d):
+        return [
+            (i, i // x_size * x_size + (i % x_size + d) % x_size) for i in range(dp_size)
+        ]
+
+    def z_turn(d):
+        return [(i, (i // x_size + d) % z_size * x_size + i % x_size) for i in range(dp_size)]
+
+    widened = jnp.tile(weight_rows, (WIDEN, 1))
+    kv_theirs, widened = lax.optimization_barrier((kv_theirs, widened))
+    weight_block = (
+        lax.all_gather(widened, "dp", axis=0, tiled=True)
+        .reshape(dp_size, WIDEN, rows_dev, weight_rows.shape[1])[:, 0]
+        .reshape(dp_size * rows_dev, weight_rows.shape[1])
+    )
+
     kv_got = lax.ppermute(kv_theirs, "seq", swap_cores)
     kv_own = jnp.where(
         core == 0,
@@ -299,33 +328,6 @@
         jnp.stack([own_docs, other_docs])[:, :, None] == lanes[None, None, :], 0.0, masked_bias
     ).astype(bf16)
 
-    rows_dev = weight_codes.shape[0]
-    first_global = (dp_idx * seq_size + seq_idx) * rows_dev
-    row_block = (first_global + jnp.arange(rows_dev)) // SCALE_BLOCK_SIDE
-    row_pick = (row_block[:, None] == jnp.arange(exponents.shape[0])[None, :]).astype(f32)
-    row_scale = jnp.dot(
-        row_pick, jnp.exp2(exponents.astype(f32)), precision=lax.Precision.HIGHEST
-    )
-    column_scale = jnp.repeat(row_scale, SCALE_BLOCK_SIDE, axis=1)
-    weight_rows = decode_rows(weight_codes, column_scale)
-    x_size = 4
-    x_at, z_at = dp_idx % x_size, dp_idx // x_size
-    z_size = dp_size // x_size
-
-    def x_turn(d):
-        return [
-            (i, i // x_size * x_size + (i % x_size + d) % x_size) for i in range(dp_size)
-        ]
-
-    def z_turn(d):
-        return [(i, (i // x_size + d) % z_size * x_size + i % x_size) for i in range(dp_size)]
-
-    weight_block = (
-        lax.all_gather(jnp.tile(weight_rows, (WIDEN, 1)), "dp", axis=0, tiled=True)
-        .reshape(dp_size, WIDEN, rows_dev, weight_rows.shape[1])[:, 0]
-        .reshape(dp_size * rows_dev, weight_rows.shape[1])
-    )
-
     tokens = activations.shape[0]
     piece = activations.shape[1] // (dp_size * seq_size)
     act_rows = (
@@ -355,7 +357,9 @@
             dkv_halo[d - 1], "seq", [(i, i - 2 * d) for i in range(2 * d, seq_size)]
         )
         kv_sum = kv_sum + part.astype(f32)
-    kv_chip, weight_block = lax.optimization_barrier((kv_sum.astype(bf16), weight_block))
+    kv_chip, weight_block, act_all, grad_q = lax.optimization_barrier(
+        (kv_sum.astype(bf16), weight_block, act_all, grad_q)
+    )
     kv_group = lax.all_to_all(
         jnp.broadcast_to(kv_chip[None], (chips,) + kv_chip.shape),
         "seq",
@@ -376,6 +380,7 @@
         return total
 
     blocks = weight_part.reshape(z_size, x_size, piece, weight_part.shape[1]).transpose(1, 0, 2, 3)
+    kv_group, kv_swap, blocks = lax.optimization_barrier((kv_group, kv_swap, blocks))
     in_row = ring_scatter(blocks, x_turn, x_size, x_at)
     total = ring_scatter(in_row, z_turn, z_size, z_at)
     own_k, own_v, other_k, other_v = (total[:, i * 128 : (i + 1) * 128] for i in range(4))

time: 145 us -> 139 us (0.959)
  local copies, waits for them, and re-layouts: 14.2 us -> 11.3 us
  waiting for transfers between devices: 18.8 us -> 16.5 us
    all_gather x1, waiting for transfers between devices: 12.6 us -> 0.01 us  [on_device(): lax.all_gather(widened, 'dp', axis=0, tiled=True)]
    ppermute x4, waiting for transfers between devices: 0.01 us -> 5.85 us  [on_device(): lax.ppermute(dkv_halo[d - 1], 'seq', [(i, i - 2 * d) for i in range(2 * d...]
    ppermute x4, waiting for transfers between devices: 1.13 us -> 3.7 us  [on_device(): lax.ppermute(kv_own, 'seq', [(i, i + 2 * d) for i in range(seq_size - 2 *...]
    ppermute x6, waiting for transfers between devices: 4.49 us -> 6.88 us  [ring_scatter(): total = total + lax.ppermute(block.astype(bf16), 'dp', turn(d)).astype(f32)]
    ppermute x6, starting transfers between devices: 13.5 us -> 15.7 us  [ring_scatter(): total = total + lax.ppermute(block.astype(bf16), 'dp', turn(d)).astype(f32)]
    unnamed x20 -> x18, local copies, waits for them, and re-layouts: 4.44 us -> 2.78 us
    dot_general x1 -> x0, local copies, waits for them, and re-layouts: 1.51 us -> none  [dot(): return lax.dot_general(a, b, dims, preferred_element_type=jnp.float32)]
  transfers between devices with their start and end apart: 22 -> 22, of which waited for: 7 -> 8; matrix products, arithmetic and copies ran while one was open for 15% -> 9% of each run, Pallas kernels for 15% -> 15%
where the time goes in v4:
time: 139 us; the launch traced here: 138 us
  starting transfers between devices  46.2 us (33%)
  Pallas kernels  20.8 us (15%)
  blocking collectives  19.1 us (14%)
  waiting for transfers between devices  16.5 us (12%)
  between operations  14.5 us (10%)
  local copies, waits for them, and re-layouts  11.3 us (8%)
  other arithmetic  5.83 us (4%)
  matrix products  4.08 us (3%)
    pallas_call x1, Pallas kernels, attend_grads(): pl.pallas_call(attention_kernel, grid_spec=pltpu.PrefetchScalarGridSpec(n...  20.8 us
    all_to_all x1, blocking collectives, on_device(): lax.all_to_all(jnp.broadcast_to(kv_chip[None], (chips,) + kv_chip.shape),...  19.1 us
    ppermute x6, starting transfers between devices, ring_scatter(): total = total + lax.ppermute(block.astype(bf16), 'dp', turn(d)).astype(f32)  15.7 us
    ppermute x4, starting transfers between devices, on_device(): lax.ppermute(kv_own, 'seq', [(i, i + 2 * d) for i in range(seq_size - 2 *...  11.9 us
    ppermute x4, starting transfers between devices, on_device(): lax.ppermute(dkv_halo[d - 1], 'seq', [(i, i - 2 * d) for i in range(2 * d...  7.88 us
    ppermute x6, waiting for transfers between devices, ring_scatter(): total = total + lax.ppermute(block.astype(bf16), 'dp', turn(d)).astype(f32)  6.88 us
    ppermute x4, waiting for transfers between devices, on_device(): lax.ppermute(dkv_halo[d - 1], 'seq', [(i, i - 2 * d) for i in range(2 * d...  5.85 us
    all_to_all x1, starting transfers between devices, on_device(): grad_x = lax.all_to_all(grad_x_rows, 'seq', split_axis=0, concat_axis=0)  5.33 us
  transfers between devices with their start and end apart: 22, of which 8 were waited for; matrix products, arithmetic and copies ran while one was open for 9% of the time, Pallas kernels for 15%

profile of v4, /device:TPU:8, one launch (start us, length us, event | category | flops | bytes accessed | tf_op | source)
XLA Modules:
  0.0 138.4 jit_solution(14895521047588158248)
XLA Ops:
  7.2 0.0 copy-start.2
  7.2 0.0 all-gather.2.cloned.1.call-start
  7.3 1.0 fusion.35
  8.3 0.1 broadcast_in_dim.12
  8.4 0.8 fusion.18
  9.2 0.8 constant_dynamic-slice_fusion.10
  10.1 0.6 tile.4
  10.7 0.0 all-gather.2.cloned.1.call-update
  10.7 0.1 collective-permute-start
  10.8 1.1 constant_dynamic-slice_fusion.6
  11.9 0.6 collective-permute-start.6
  12.5 0.0 collective-permute-done
  12.5 4.2 %collective-permute-start.4 = (bf16[256,256]{1,0:T(8,128)(2,1)S(1)}, bf16[256,256]{1,0:T(8,128)(2,1)S(1)}, u32[]{:S(2)}, u32[]{:S(2)}) collective-permute-start(bf16[256,256]{1,0:T(8,128)(2,1)S(1)} %maximum_select_fusion.1.kv_own), channel_id=1, source_target_pairs={{0,8},{1,9},{2,10},{3,11},{4,12},{5,13},{6,14},{7,15},{16,24},{17,... | collective-permute-start | bytes 393224 | tf_op jit(solution)/shard_map/ppermute | solution.py:314
  16.7 1.9 %collective-permute-start.3 = (bf16[256,256]{1,0:T(8,128)(2,1)S(1)}, bf16[256,256]{1,0:T(8,128)(2,1)S(1)}, u32[]{:S(2)}, u32[]{:S(2)}) collective-permute-start(bf16[256,256]{1,0:T(8,128)(2,1)S(1)} %maximum_select_fusion.1.kv_own), channel_id=1, source_target_pairs={{0,6},{1,7},{2,8},{3,9},{4,10},{5,11},{6,12},{7,13},{8,14},{9,15},... | collective-permute-start | bytes 393224 | tf_op jit(solution)/shard_map/ppermute | solution.py:314
  18.7 3.2 %collective-permute-start.2 = (bf16[256,256]{1,0:T(8,128)(2,1)S(1)}, bf16[256,256]{1,0:T(8,128)(2,1)}, u32[]{:S(2)}, u32[]{:S(2)}) collective-permute-start(bf16[256,256]{1,0:T(8,128)(2,1)S(1)} %maximum_select_fusion.1.kv_own), channel_id=1, source_target_pairs={{0,4},{1,5},{2,6},{3,7},{4,8},{5,9},{6,10},{7,11},{8,12},{9,13},{1... | collective-permute-start | bytes 393224 | tf_op jit(solution)/shard_map/ppermute | solution.py:314
  21.9 2.6 %collective-permute-start.1 = (bf16[256,256]{1,0:T(8,128)(2,1)S(1)}, bf16[256,256]{1,0:T(8,128)(2,1)}, u32[]{:S(2)}, u32[]{:S(2)}) collective-permute-start(bf16[256,256]{1,0:T(8,128)(2,1)S(1)} %maximum_select_fusion.1.kv_own), channel_id=1, source_target_pairs={{0,2},{1,3},{2,4},{3,5},{4,6},{5,7},{6,8},{7,9},{8,10},{9,11},{10,... | collective-permute-start | bytes 393224 | tf_op jit(solution)/shard_map/ppermute | solution.py:314
  24.5 0.0 copy-start.4
  24.5 0.7 copy.25
  25.2 1.2 copy.26
  26.4 0.1 pad_dynamic-slice_fusion
  26.5 0.0 collective-permute-done.4.kv_4
  26.5 0.0 collective-permute-start.5
  26.6 0.0 collective-permute-done.3.kv_3
  26.6 2.9 %collective-permute-done.2.kv_2 = bf16[256,256]{1,0:T(8,128)(2,1)} collective-permute-done((bf16[256,256]{1,0:T(8,128)(2,1)S(1)}, bf16[256,256]{1,0:T(8,128)(2,1)}, u32[]{:S(2)}, u32[]{:S(2)}) %collective-permute-start.2) | collective-permute-done | bytes 131104 | tf_op jit(solution)/shard_map/ppermute | solution.py:314
  29.5 0.8 collective-permute-done.1.kv_1
  30.3 4.5 %all-to-all-start = ((bf16[16,256,128]{2,1,0:T(8,128)(2,1)}), bf16[16,256,128]{2,1,0:T(8,128)(2,1)S(1)}, u32[]{:S(2)}, u32[]{:S(2)}) async-start(bf16[16,256,128]{2,1,0:T(8,128)(2,1)} %bitcast.3), calls=%async_computation | async-start | bytes 2097152 | tf_op jit(solution)/shard_map/all_to_all | solution.py:339
  34.8 1.0 fusion.2.key_mark
  35.8 0.7 select_convert_fusion.query_mark
  36.6 0.8 copy-done.5
  37.3 20.8 %shard_map.103 = (bf16[128,2048]{1,0:T(8,128)(2,1)}, bf16[128,2048]{1,0:T(8,128)(2,1)}, bf16[256,256]{1,0:T(8,128)(2,1)}, bf16[256,256]{1,0:T(8,128)(2,1)}, bf16...) custom-call(s32[1]{0:T(128)} %bitcast.5.core_ref, bf16[128,4096]{1,0:T(8,128)(2,1)} %q_own.1, ...), custom_call_target="tpu_custom_call" | custom-call | flops 7247757312 | bytes 5242880 | tf_op jit(solution)/shard_map/pallas_call | solution.py:188
  58.2 0.2 collective-permute-start.11
  58.4 3.4 %collective-permute-start.7 = (bf16[256,256]{1,0:T(8,128)(2,1)}, bf16[256,256]{1,0:T(8,128)(2,1)S(1)}, u32[]{:S(2)}, u32[]{:S(2)}) collective-permute-start(bf16[256,256]{1,0:T(8,128)(2,1)} %get-tuple-element.42), channel_id=1, source_target_pairs={{2,0},{3,1},{4,2},{5,3},{6,4},{7,5},{8,6},{9,7},{10,8},{11,9},{12,... | collective-permute-start | bytes 393224 | tf_op jit(solution)/shard_map/ppermute | solution.py:356
  61.8 1.9 %collective-permute-start.8 = (bf16[256,256]{1,0:T(8,128)(2,1)}, bf16[256,256]{1,0:T(8,128)(2,1)S(1)}, u32[]{:S(2)}, u32[]{:S(2)}) collective-permute-start(bf16[256,256]{1,0:T(8,128)(2,1)} %get-tuple-element.43), channel_id=1, source_target_pairs={{4,0},{5,1},{6,2},{7,3},{8,4},{9,5},{10,6},{11,7},{12,8},{13,9},{1... | collective-permute-start | bytes 393224 | tf_op jit(solution)/shard_map/ppermute | solution.py:356
  63.7 1.3 collective-permute-start.9
  65.0 1.3 collective-permute-start.10
  66.3 2.5 %maximum_select_fusion = bf16[128,4096]{1,0:T(8,128)(2,1)} fusion(bf16[128,2048]{1,0:T(8,128)(2,1)S(1)} %collective-permute-done.11, bf16[128,2048]{1,0:T(8,128)(2,1)} %get-tuple-element.48, pred[]{:T(512)S(6)} %eq.56), kind=kLoop, calls=%fused_computation.6 | loop fusion | flops 4718592 | bytes 2097153 | tf_op jit(solution)/shard_map/jit(_where)/select_n | solution.py:346
  68.8 1.0 slice.20
  69.8 0.5 copy.28
  70.3 2.0 %collective-permute-done.9 = bf16[256,256]{1,0:T(8,128)(2,1)S(1)} collective-permute-done((bf16[256,256]{1,0:T(8,128)(2,1)}, bf16[256,256]{1,0:T(8,128)(2,1)S(1)}, u32[]{:S(2)}, u32[]{:S(2)}) %collective-permute-start.9) | collective-permute-done | bytes 131104 | tf_op jit(solution)/shard_map/ppermute | solution.py:356
  72.3 3.9 %collective-permute-done.10 = bf16[256,256]{1,0:T(8,128)(2,1)S(1)} collective-permute-done((bf16[256,256]{1,0:T(8,128)(2,1)}, bf16[256,256]{1,0:T(8,128)(2,1)S(1)}, u32[]{:S(2)}, u32[]{:S(2)}) %collective-permute-start.10) | collective-permute-done | bytes 131104 | tf_op jit(solution)/shard_map/ppermute | solution.py:356
  76.2 0.1 add_convert_fusion
  76.2 0.1 broadcast_in_dim.15
  76.3 19.1 %all_to_all.15 = bf16[8,256,256]{2,1,0:T(8,128)(2,1)S(1)} all-to-all(bf16[8,256,256]{2,1,0:T(8,128)(2,1)S(1)} %broadcast_in_dim.15), channel_id=1, replica_groups={{0,2,4,6,8,10,12,14},{1,3,5,7,9,11,13,15},{16,18,20,22,24,26,28,30},{17..., dimensions={0} | all-to-all | bytes 2097152 | tf_op jit(solution)/shard_map/all_to_all | solution.py:363
  95.5 0.0 collective-permute-start.12
  95.5 1.4 %copy.29 = bf16[256,2048]{1,0:T(8,128)(2,1)} copy(bf16[256,2048]{0,1:T(8,128)(2,1)S(1)} %bitcast.66) | data formatting | bytes 2097152 | tf_op jit(solution)/shard_map/optimization_barrier | solution.py:360
  96.9 1.7 %convolution_convert_fusion.1 = bf16[4,4,16,256]{3,2,1,0:T(8,128)(2,1)S(1)} fusion(bf16[4,4,16,2048]{3,2,1,0:T(8,128)(2,1)} %bitcast.73, bf16[2048,256,1,1]{1,0,3,2:T(8,128)(2,1)S(1)} %bitcast.69), kind=kOutput, calls=%fused_computation.4 | convolution fusion | flops 268500992 | bytes 2228224 | tf_op jit(solution)/shard_map/dot_general | solution.py:30
  98.6 0.5 convolution_convert_fusion
  99.1 0.5 fusion.6
  99.6 0.5 fusion.1
  100.1 1.2 copy.39
  101.3 5.3 %all-to-all-start.2 = ((bf16[16,256,128]{2,1,0:T(8,128)(2,1)}), bf16[16,256,128]{2,1,0:T(8,128)(2,1)S(1)}, u32[]{:S(2)}, u32[]{:S(2)}) async-start(bf16[16,256,128]{2,1,0:T(8,128)(2,1)} %bitcast.65), calls=%async_computation.2 | async-start | bytes 2097152 | tf_op jit(solution)/shard_map/all_to_all | solution.py:401
  106.7 1.4 %collective-permute-start.13 = (bf16[4,16,512]{2,1,0:T(8,128)(2,1)S(1)}, bf16[4,16,512]{2,1,0:T(8,128)(2,1)S(1)}, u32[]{:S(2)}, u32[]{:S(2)}) collective-permute-start(bf16[4,16,512]{2,1,0:T(8,128)(2,1)S(1)} %get-tuple-element.66), channel_id=1, source_target_pairs={{0,16},{16,32},{32,48},{48,0},{64,80},{80,96},{96,112},{112,64},{1... | collective-permute-start | bytes 196616 | tf_op jit(solution)/shard_map/ppermute | solution.py:379
  108.1 1.9 %collective-permute-start.15 = (bf16[4,16,512]{2,1,0:T(8,128)(2,1)S(1)}, bf16[4,16,512]{2,1,0:T(8,128)(2,1)S(1)}, u32[]{:S(2)}, u32[]{:S(2)}) collective-permute-start(bf16[4,16,512]{2,1,0:T(8,128)(2,1)S(1)} %get-tuple-element.67), channel_id=1, source_target_pairs={{0,48},{16,0},{32,16},{48,32},{64,112},{80,64},{96,80},{112,96},{1... | collective-permute-start | bytes 196616 | tf_op jit(solution)/shard_map/ppermute | solution.py:379
  110.0 1.6 %collective-permute-start.14 = (bf16[4,16,512]{2,1,0:T(8,128)(2,1)S(1)}, bf16[4,16,512]{2,1,0:T(8,128)(2,1)S(1)}, u32[]{:S(2)}, u32[]{:S(2)}) collective-permute-start(bf16[4,16,512]{2,1,0:T(8,128)(2,1)S(1)} %get-tuple-element.68), channel_id=1, source_target_pairs={{0,32},{16,48},{32,0},{48,16},{64,96},{80,112},{96,64},{112,80},{1... | collective-permute-start | bytes 196616 | tf_op jit(solution)/shard_map/ppermute | solution.py:379
  111.6 0.6 collective-permute-done.13
  112.2 0.3 collective-permute-done.15
  112.5 3.3 %collective-permute-done.14 = bf16[4,16,512]{2,1,0:T(8,128)(2,1)S(1)} collective-permute-done((bf16[4,16,512]{2,1,0:T(8,128)(2,1)S(1)}, bf16[4,16,512]{2,1,0:T(8,128)(2,1)S(1)}, u32[]{:S(2)}, u32[]{:S(2)}) %collective-permute-start.14) | collective-permute-done | bytes 65568 | tf_op jit(solution)/shard_map/ppermute | solution.py:379
  115.8 2.7 %collective-permute-start.16 = (bf16[16,512]{1,0:T(8,128)(2,1)S(1)}, bf16[16,512]{1,0:T(8,128)(2,1)S(1)}, u32[]{:S(2)}, u32[]{:S(2)}) collective-permute-start(bf16[16,512]{1,0:T(8,128)(2,1)S(1)} %get-tuple-element.73), channel_id=1, source_target_pairs={{0,64},{16,80},{32,96},{48,112},{64,128},{80,144},{96,160},{112,17... | collective-permute-start | bytes 49160 | tf_op jit(solution)/shard_map/ppermute | solution.py:379
  118.5 3.1 %collective-permute-start.18 = (bf16[16,512]{1,0:T(8,128)(2,1)S(1)}, bf16[16,512]{1,0:T(8,128)(2,1)S(1)}, u32[]{:S(2)}, u32[]{:S(2)}) collective-permute-start(bf16[16,512]{1,0:T(8,128)(2,1)S(1)} %get-tuple-element.74), channel_id=1, source_target_pairs={{0,192},{16,208},{32,224},{48,240},{64,0},{80,16},{96,32},{112,48}... | collective-permute-start | bytes 49160 | tf_op jit(solution)/shard_map/ppermute | solution.py:379
  121.6 4.9 %collective-permute-start.17 = (bf16[16,512]{1,0:T(8,128)(2,1)S(1)}, bf16[16,512]{1,0:T(8,128)(2,1)S(1)}, u32[]{:S(2)}, u32[]{:S(2)}) collective-permute-start(bf16[16,512]{1,0:T(8,128)(2,1)S(1)} %get-tuple-element.75), channel_id=1, source_target_pairs={{0,128},{16,144},{32,160},{48,176},{64,192},{80,208},{96,224},{112... | collective-permute-start | bytes 49160 | tf_op jit(solution)/shard_map/ppermute | solution.py:379
  126.6 2.7 %collective-permute-done.17 = bf16[16,512]{1,0:T(8,128)(2,1)S(1)} collective-permute-done((bf16[16,512]{1,0:T(8,128)(2,1)S(1)}, bf16[16,512]{1,0:T(8,128)(2,1)S(1)}, u32[]{:S(2)}, u32[]{:S(2)}) %collective-permute-start.17) | collective-permute-done | bytes 16416 | tf_op jit(solution)/shard_map/ppermute | solution.py:379
  129.3 0.6 maximum_select_fusion.2
  129.9 0.3 copy.31
  130.2 1.3 copy.32
  (37 shorter events, 0.3 us)
Async XLA Ops:
  7.2 17.3 %copy-start.2 = (bf16[128,4096]{1,0:T(8,128)(2,1)S(1)}, bf16[128,4096]{1,0:T(8,128)(2,1)}, u32[]{:S(2)}) copy-start(bf16[128,4096]{1,0:T(8,128)(2,1)} %q_own.1) | copy-start | bytes 3145732
  7.2 17.3 %copy-start = (bf16[128,4096]{1,0:T(8,128)(2,1)S(1)}, bf16[128,4096]{1,0:T(8,128)(2,1)}, u32[]{:S(2)}) copy-start(bf16[128,4096]{1,0:T(8,128)(2,1)} %param.8) | copy-start | bytes 3145732
  7.2 61.6 %all-gather.2.cloned.1.call-start = ((), (), s32[]{:S(2)}) async-start(), calls=%async_computation.3 | async-start | bytes 1114112 | tf_op jit(solution)/shard_map/all_gather | solution.py:302
  10.7 1.8 %collective-permute-start = (bf16[128,256]{1,0:T(8,128)(2,1)S(1)}, bf16[128,256]{1,0:T(8,128)(2,1)S(1)}, u32[]{:S(2)}, u32[]{:S(2)}) collective-permute-start(bf16[128,256]{1,0:T(8,128)(2,1)S(1)} %pad_maximum_fusion), channel_id=1, source_target_pairs={{0,1},{1,0},{2,3},{3,2},{4,5},{5,4},{6,7},{7,6},{8,9},{9,8},{10,11... | collective-permute-start | bytes 196616 | tf_op jit(solution)/shard_map/ppermute | solution.py:307
  11.9 24.6 %collective-permute-start.6 = (bf16[128,2048]{1,0:T(8,128)(2,1)S(1)}, bf16[128,2048]{1,0:T(8,128)(2,1)}, u32[]{:S(2)}, u32[]{:S(2)}) collective-permute-start(bf16[128,2048]{1,0:T(8,128)(2,1)S(1)} %constant_dynamic-slice_fusion.6), channel_id=1, source_target_pairs={{0,1},{1,0},{2,3},{3,2},{4,5},{5,4},{6,7},{7,6},{8,9},{9,8},{10,11... | collective-permute-start | bytes 1572872 | tf_op jit(solution)/shard_map/ppermute | solution.py:318
  12.5 13.9 %copy-start.3 = (bf16[256,256]{1,0:T(8,128)(2,1)}, bf16[256,256]{1,0:T(8,128)(2,1)S(1)}, u32[]{:S(2)}) copy-start(bf16[256,256]{1,0:T(8,128)(2,1)S(1)} %maximum_select_fusion.1.kv_own) | copy-start | bytes 393220
  12.5 14.0 %collective-permute-start.4 = (bf16[256,256]{1,0:T(8,128)(2,1)S(1)}, bf16[256,256]{1,0:T(8,128)(2,1)S(1)}, u32[]{:S(2)}, u32[]{:S(2)}) collective-permute-start(bf16[256,256]{1,0:T(8,128)(2,1)S(1)} %maximum_select_fusion.1.kv_own), channel_id=1, source_target_pairs={{0,8},{1,9},{2,10},{3,11},{4,12},{5,13},{6,14},{7,15},{16,24},{17,... | collective-permute-start | bytes 393224 | tf_op jit(solution)/shard_map/ppermute | solution.py:314
  16.7 9.9 %collective-permute-start.3 = (bf16[256,256]{1,0:T(8,128)(2,1)S(1)}, bf16[256,256]{1,0:T(8,128)(2,1)S(1)}, u32[]{:S(2)}, u32[]{:S(2)}) collective-permute-start(bf16[256,256]{1,0:T(8,128)(2,1)S(1)} %maximum_select_fusion.1.kv_own), channel_id=1, source_target_pairs={{0,6},{1,7},{2,8},{3,9},{4,10},{5,11},{6,12},{7,13},{8,14},{9,15},... | collective-permute-start | bytes 393224 | tf_op jit(solution)/shard_map/ppermute | solution.py:314
  18.7 10.8 %collective-permute-start.2 = (bf16[256,256]{1,0:T(8,128)(2,1)S(1)}, bf16[256,256]{1,0:T(8,128)(2,1)}, u32[]{:S(2)}, u32[]{:S(2)}) collective-permute-start(bf16[256,256]{1,0:T(8,128)(2,1)S(1)} %maximum_select_fusion.1.kv_own), channel_id=1, source_target_pairs={{0,4},{1,5},{2,6},{3,7},{4,8},{5,9},{6,10},{7,11},{8,12},{9,13},{1... | collective-permute-start | bytes 393224 | tf_op jit(solution)/shard_map/ppermute | solution.py:314
  21.9 8.4 %collective-permute-start.1 = (bf16[256,256]{1,0:T(8,128)(2,1)S(1)}, bf16[256,256]{1,0:T(8,128)(2,1)}, u32[]{:S(2)}, u32[]{:S(2)}) collective-permute-start(bf16[256,256]{1,0:T(8,128)(2,1)S(1)} %maximum_select_fusion.1.kv_own), channel_id=1, source_target_pairs={{0,2},{1,3},{2,4},{3,5},{4,6},{5,7},{6,8},{7,9},{8,10},{9,11},{10,... | collective-permute-start | bytes 393224 | tf_op jit(solution)/shard_map/ppermute | solution.py:314
  24.5 1.9 %copy-start.4 = (s32[1,2048]{1,0:T(1,128)S(1)}, s32[1,2048]{1,0:T(1,128)}, u32[]{:S(2)}) copy-start(s32[1,2048]{1,0:T(1,128)} %param.13) | copy-start | bytes 24580
  26.5 10.0 %copy-start.6 = (bf16[256,256]{1,0:T(8,128)(2,1)}, bf16[256,256]{1,0:T(8,128)(2,1)S(1)}, u32[]{:S(2)}) copy-start(bf16[256,256]{1,0:T(8,128)(2,1)S(1)} %collective-permute-done.4.kv_4) | copy-start | bytes 393220
  26.5 10.0 %collective-permute-start.5 = (bf16[128,2048]{1,0:T(8,128)(2,1)S(1)}, bf16[128,2048]{1,0:T(8,128)(2,1)S(1)}, u32[]{:S(2)}, u32[]{:S(2)}) collective-permute-start(bf16[128,2048]{1,0:T(8,128)(2,1)S(1)} %constant_dynamic-slice_fusion.7), channel_id=1, source_target_pairs={{0,1},{1,0},{2,3},{3,2},{4,5},{5,4},{6,7},{7,6},{8,9},{9,8},{10,11... | collective-permute-start | bytes 1572872 | tf_op jit(solution)/shard_map/ppermute | solution.py:317
  26.6 10.0 %copy-start.7 = (bf16[256,256]{1,0:T(8,128)(2,1)}, bf16[256,256]{1,0:T(8,128)(2,1)S(1)}, u32[]{:S(2)}) copy-start(bf16[256,256]{1,0:T(8,128)(2,1)S(1)} %collective-permute-done.3.kv_3) | copy-start | bytes 393220
  30.3 28.1 %all-to-all-start = ((bf16[16,256,128]{2,1,0:T(8,128)(2,1)}), bf16[16,256,128]{2,1,0:T(8,128)(2,1)S(1)}, u32[]{:S(2)}, u32[]{:S(2)}) async-start(bf16[16,256,128]{2,1,0:T(8,128)(2,1)} %bitcast.3), calls=%async_computation | async-start | bytes 2097152 | tf_op jit(solution)/shard_map/all_to_all | solution.py:339
  36.5 0.8 copy-start.5
  58.2 8.1 %collective-permute-start.11 = (bf16[128,2048]{1,0:T(8,128)(2,1)}, bf16[128,2048]{1,0:T(8,128)(2,1)S(1)}, u32[]{:S(2)}, u32[]{:S(2)}) collective-permute-start(bf16[128,2048]{1,0:T(8,128)(2,1)} %get-tuple-element.49), channel_id=1, source_target_pairs={{0,1},{1,0},{2,3},{3,2},{4,5},{5,4},{6,7},{7,6},{8,9},{9,8},{10,11... | collective-permute-start | bytes 1572872 | tf_op jit(solution)/shard_map/ppermute | solution.py:345
  58.4 11.9 %collective-permute-start.7 = (bf16[256,256]{1,0:T(8,128)(2,1)}, bf16[256,256]{1,0:T(8,128)(2,1)S(1)}, u32[]{:S(2)}, u32[]{:S(2)}) collective-permute-start(bf16[256,256]{1,0:T(8,128)(2,1)} %get-tuple-element.42), channel_id=1, source_target_pairs={{2,0},{3,1},{4,2},{5,3},{6,4},{7,5},{8,6},{9,7},{10,8},{11,9},{12,... | collective-permute-start | bytes 393224 | tf_op jit(solution)/shard_map/ppermute | solution.py:356
  61.8 8.5 %collective-permute-start.8 = (bf16[256,256]{1,0:T(8,128)(2,1)}, bf16[256,256]{1,0:T(8,128)(2,1)S(1)}, u32[]{:S(2)}, u32[]{:S(2)}) collective-permute-start(bf16[256,256]{1,0:T(8,128)(2,1)} %get-tuple-element.43), channel_id=1, source_target_pairs={{4,0},{5,1},{6,2},{7,3},{8,4},{9,5},{10,6},{11,7},{12,8},{13,9},{1... | collective-permute-start | bytes 393224 | tf_op jit(solution)/shard_map/ppermute | solution.py:356
  63.7 8.6 %collective-permute-start.9 = (bf16[256,256]{1,0:T(8,128)(2,1)}, bf16[256,256]{1,0:T(8,128)(2,1)S(1)}, u32[]{:S(2)}, u32[]{:S(2)}) collective-permute-start(bf16[256,256]{1,0:T(8,128)(2,1)} %get-tuple-element.44), channel_id=1, source_target_pairs={{6,0},{7,1},{8,2},{9,3},{10,4},{11,5},{12,6},{13,7},{14,8},{15,9},... | collective-permute-start | bytes 393224 | tf_op jit(solution)/shard_map/ppermute | solution.py:356
  65.0 11.2 %collective-permute-start.10 = (bf16[256,256]{1,0:T(8,128)(2,1)}, bf16[256,256]{1,0:T(8,128)(2,1)S(1)}, u32[]{:S(2)}, u32[]{:S(2)}) collective-permute-start(bf16[256,256]{1,0:T(8,128)(2,1)} %get-tuple-element.45), channel_id=1, source_target_pairs={{8,0},{9,1},{10,2},{11,3},{12,4},{13,5},{14,6},{15,7},{24,16},{25,... | collective-permute-start | bytes 393224 | tf_op jit(solution)/shard_map/ppermute | solution.py:356
  66.3 9.8 %copy-start.1 = (f32[256,256]{1,0:T(8,128)S(1)}, f32[256,256]{1,0:T(8,128)}, u32[]{:S(2)}) copy-start(f32[256,256]{1,0:T(8,128)} %get-tuple-element.41) | copy-start | bytes 786436
  95.5 3.1 %collective-permute-start.12 = (bf16[2048,256]{1,0:T(8,128)(2,1)S(1)}, bf16[2048,256]{1,0:T(8,128)(2,1)S(1)}, u32[]{:S(2)}, u32[]{:S(2)}) collective-permute-start(bf16[2048,256]{1,0:T(8,128)(2,1)S(1)} %bitcast.68), channel_id=1, source_target_pairs={{0,1},{1,0},{2,3},{3,2},{4,5},{5,4},{6,7},{7,6},{8,9},{9,8},{10,11... | collective-permute-start | bytes 3145736 | tf_op jit(solution)/shard_map/ppermute | solution.py:370
  101.3 28.6 %all-to-all-start.2 = ((bf16[16,256,128]{2,1,0:T(8,128)(2,1)}), bf16[16,256,128]{2,1,0:T(8,128)(2,1)S(1)}, u32[]{:S(2)}, u32[]{:S(2)}) async-start(bf16[16,256,128]{2,1,0:T(8,128)(2,1)} %bitcast.65), calls=%async_computation.2 | async-start | bytes 2097152 | tf_op jit(solution)/shard_map/all_to_all | solution.py:401
  106.7 5.6 %collective-permute-start.13 = (bf16[4,16,512]{2,1,0:T(8,128)(2,1)S(1)}, bf16[4,16,512]{2,1,0:T(8,128)(2,1)S(1)}, u32[]{:S(2)}, u32[]{:S(2)}) collective-permute-start(bf16[4,16,512]{2,1,0:T(8,128)(2,1)S(1)} %get-tuple-element.66), channel_id=1, source_target_pairs={{0,16},{16,32},{32,48},{48,0},{64,80},{80,96},{96,112},{112,64},{1... | collective-permute-start | bytes 196616 | tf_op jit(solution)/shard_map/ppermute | solution.py:379
  108.1 4.4 %collective-permute-start.15 = (bf16[4,16,512]{2,1,0:T(8,128)(2,1)S(1)}, bf16[4,16,512]{2,1,0:T(8,128)(2,1)S(1)}, u32[]{:S(2)}, u32[]{:S(2)}) collective-permute-start(bf16[4,16,512]{2,1,0:T(8,128)(2,1)S(1)} %get-tuple-element.67), channel_id=1, source_target_pairs={{0,48},{16,0},{32,16},{48,32},{64,112},{80,64},{96,80},{112,96},{1... | collective-permute-start | bytes 196616 | tf_op jit(solution)/shard_map/ppermute | solution.py:379
  110.0 5.8 %collective-permute-start.14 = (bf16[4,16,512]{2,1,0:T(8,128)(2,1)S(1)}, bf16[4,16,512]{2,1,0:T(8,128)(2,1)S(1)}, u32[]{:S(2)}, u32[]{:S(2)}) collective-permute-start(bf16[4,16,512]{2,1,0:T(8,128)(2,1)S(1)} %get-tuple-element.68), channel_id=1, source_target_pairs={{0,32},{16,48},{32,0},{48,16},{64,96},{80,112},{96,64},{112,80},{1... | collective-permute-start | bytes 196616 | tf_op jit(solution)/shard_map/ppermute | solution.py:379
  115.8 10.7 %collective-permute-start.16 = (bf16[16,512]{1,0:T(8,128)(2,1)S(1)}, bf16[16,512]{1,0:T(8,128)(2,1)S(1)}, u32[]{:S(2)}, u32[]{:S(2)}) collective-permute-start(bf16[16,512]{1,0:T(8,128)(2,1)S(1)} %get-tuple-element.73), channel_id=1, source_target_pairs={{0,64},{16,80},{32,96},{48,112},{64,128},{80,144},{96,160},{112,17... | collective-permute-start | bytes 49160 | tf_op jit(solution)/shard_map/ppermute | solution.py:379
  118.5 8.0 %collective-permute-start.18 = (bf16[16,512]{1,0:T(8,128)(2,1)S(1)}, bf16[16,512]{1,0:T(8,128)(2,1)S(1)}, u32[]{:S(2)}, u32[]{:S(2)}) collective-permute-start(bf16[16,512]{1,0:T(8,128)(2,1)S(1)} %get-tuple-element.74), channel_id=1, source_target_pairs={{0,192},{16,208},{32,224},{48,240},{64,0},{80,16},{96,32},{112,48}... | collective-permute-start | bytes 49160 | tf_op jit(solution)/shard_map/ppermute | solution.py:379
  121.6 7.6 %collective-permute-start.17 = (bf16[16,512]{1,0:T(8,128)(2,1)S(1)}, bf16[16,512]{1,0:T(8,128)(2,1)S(1)}, u32[]{:S(2)}, u32[]{:S(2)}) collective-permute-start(bf16[16,512]{1,0:T(8,128)(2,1)S(1)} %get-tuple-element.75), channel_id=1, source_target_pairs={{0,128},{16,144},{32,160},{48,176},{64,192},{80,208},{96,224},{112... | collective-permute-start | bytes 49160 | tf_op jit(solution)/shard_map/ppermute | solution.py:379
Sparse Core Ops, SparseCore 0:
  10.8 56.7 all-gather.1
